TPU v7x, 32 devices: a whole 2x2x4 slice. The times are simulated.
32 devices in a mesh: batch: 4 (over y, x), seq: 2 (over core), fsdp: 4 (over z).
Axes of the slice: x: 2, y: 2, z: 4, core: 2. Of those that a mesh axis runs over, the one named last changes fastest.
Arguments:
- tokens: bfloat16 [16, 1024, 2048], P(('batch', 'fsdp'), 'seq'), may hold values from -6 to 6
- layer_inputs: bfloat16 [16, 1024, 256], P(('batch', 'fsdp'), 'seq'), may hold values from -6 to 6
- cotangent: bfloat16 [16, 1024, 2048], P(('batch', 'fsdp'), 'seq'), may hold values from -6 to 6
- doc_lengths: int32 [16, 4], P(('batch', 'fsdp')), may hold values from 1 to 1021, as said below
- w_query: bfloat16 [2048, 2048], P(('batch', 'seq', 'fsdp')), may hold values from -0.125 to 0.125
- w_key: bfloat16 [2048, 512], P(('batch', 'seq', 'fsdp')), may hold values from -0.125 to 0.125
- w_value: bfloat16 [2048, 512], P(('batch', 'seq', 'fsdp')), may hold values from -0.125 to 0.125
- w_output: bfloat16 [2048, 2048], P(('batch', 'seq', 'fsdp')), may hold values from -0.125 to 0.125
- laurel_left: bfloat16 [2048, 64], P(('batch', 'seq', 'fsdp')), may hold values from -0.125 to 0.125
- laurel_right: bfloat16 [2048, 64], P(('batch', 'seq', 'fsdp')), may hold values from -0.75 to 0.75
- w_gate: bfloat16 [2048, 8192], P(('batch', 'seq', 'fsdp')), may hold values from -0.125 to 0.125
- w_up: bfloat16 [2048, 8192], P(('batch', 'seq', 'fsdp')), may hold values from -0.125 to 0.125
- w_down: bfloat16 [2048, 8192], P(('batch', 'seq', 'fsdp')), may hold values from -0.0625 to 0.0625
- w_plgate: bfloat16 [2048, 256], P(('batch', 'seq', 'fsdp')), may hold values from -0.125 to 0.125
- w_plproj: bfloat16 [2048, 256], P(('batch', 'seq', 'fsdp')), may hold values from -0.375 to 0.375
- g_input: bfloat16 [2048], P(('batch', 'seq', 'fsdp')), may hold values from 0.25 to 1.75
- g_query: bfloat16 [256], P(('batch', 'seq', 'fsdp')), may hold values from 0.25 to 1.75
- g_key: bfloat16 [256], P(('batch', 'seq', 'fsdp')), may hold values from 0.25 to 1.75
- g_attn: bfloat16 [2048], P(('batch', 'seq', 'fsdp')), may hold values from 0.25 to 1.75
- g_laurel: bfloat16 [2048], P(('batch', 'seq', 'fsdp')), may hold values from 0.25 to 1.75
- g_preffw: bfloat16 [2048], P(('batch', 'seq', 'fsdp')), may hold values from 0.25 to 1.75
- g_ffw: bfloat16 [2048], P(('batch', 'seq', 'fsdp')), may hold values from 0.25 to 1.75
- g_perlayer: bfloat16 [2048], P(('batch', 'seq', 'fsdp')), may hold values from 0.25 to 1.75
Outputs:
- mixed: bfloat16 [16, 1024, 2048], P(('batch', 'fsdp'), 'seq')
- grad_tokens: float32 [16, 1024, 2048], P(('batch', 'fsdp'), 'seq')
- grad_query: float32 [2048, 2048], P(('batch', 'seq', 'fsdp'))
- grad_key: float32 [2048, 512], P(('batch', 'seq', 'fsdp'))
- grad_value: float32 [2048, 512], P(('batch', 'seq', 'fsdp'))
- grad_output: float32 [2048, 2048], P(('batch', 'seq', 'fsdp'))
- grad_left: float32 [2048, 64], P(('batch', 'seq', 'fsdp'))
- grad_right: float32 [2048, 64], P(('batch', 'seq', 'fsdp'))
- grad_gate: float32 [2048, 8192], P(('batch', 'seq', 'fsdp'))
- grad_up: float32 [2048, 8192], P(('batch', 'seq', 'fsdp'))
- grad_down: float32 [2048, 8192], P(('batch', 'seq', 'fsdp'))
- grad_plgate: float32 [2048, 256], P(('batch', 'seq', 'fsdp'))
- grad_plproj: float32 [2048, 256], P(('batch', 'seq', 'fsdp'))
- grad_g_input: float32 [2048], P(('batch', 'seq', 'fsdp'))
- grad_g_query: float32 [256], P(('batch', 'seq', 'fsdp'))
- grad_g_key: float32 [256], P(('batch', 'seq', 'fsdp'))
- grad_g_attn: float32 [2048], P(('batch', 'seq', 'fsdp'))
- grad_g_laurel: float32 [2048], P(('batch', 'seq', 'fsdp'))
- grad_g_preffw: float32 [2048], P(('batch', 'seq', 'fsdp'))
- grad_g_ffw: float32 [2048], P(('batch', 'seq', 'fsdp'))
- grad_g_perlayer: float32 [2048], P(('batch', 'seq', 'fsdp'))
Inputs may be any that keep to these rules, and one draw needn't show every extreme that they name: `doc_lengths`: each row holds the lengths of 4 documents packed in order into one sequence; they sum to 1024. The first is under 512, the last two are under 512 // 2. In one row, drawn from the seed, the first and the last two are 1 and the second is 1021.
All inputs are finite; a program needn't handle non-finite values.
Results may differ from a plain program's by a relative error of at most 0.02.
Values may be sent and summed in bfloat16 or wider, within the bound.
A program may use at most 704 MiB of HBM per device.

v0:
```python
import jax
import jax.numpy as jnp
from jax import lax
from jax.sharding import PartitionSpec as P

WINDOW = 512


EPS = 1e-06
THETA = 10000.0
ROOT_HALF = 0.7071067811865476


def shifted(array, axis, by):
    count = lax.axis_size(axis)
    pairs = [(i, i + by) for i in range(count) if 0 <= i + by < count]
    return lax.ppermute(array, axis, pairs)


def rms_norm(values, weight):
    return values * lax.rsqrt(jnp.mean(values * values, -1, keepdims=True) + EPS) * weight


def norm_back(values, weight, upstream):
    normed, pull = jax.vjp(rms_norm, values, weight)
    return pull(upstream)


def geglu(gate_in, factor):
    return jax.nn.gelu(gate_in, approximate=True) * factor


def positions_of(places, lengths):
    doc_ends = jnp.cumsum(lengths)
    starts = doc_ends - lengths
    segment = jnp.sum((places[:, None] >= doc_ends[None, :]).astype(jnp.int32), 1)
    chosen = segment[:, None] == jnp.arange(lengths.shape[0], dtype=jnp.int32)[None, :]
    offset = jnp.sum(jnp.where(chosen, starts[None, :], 0), 1)
    return (segment, (places - offset).astype(jnp.float32))


def rope_tables(rel_pos, width_all):
    half_width = width_all // 2
    frequency = THETA ** (-jnp.arange(half_width, dtype=jnp.float32) * 2.0 / width_all)
    angles = rel_pos[:, None] * frequency[None, :]
    return (jnp.cos(angles)[:, None, :], jnp.sin(angles)[:, None, :])


def rotate(values, cosine_table, sine_table):
    half_width = values.shape[-1] // 2
    leading = values[..., :half_width]
    trailing = values[..., half_width:]
    return jnp.concatenate(
        [
            leading * cosine_table - trailing * sine_table,
            trailing * cosine_table + leading * sine_table,
        ],
        -1,
    )


def rotate_back(upstream, cosine_table, sine_table):
    half_width = upstream.shape[-1] // 2
    leading = upstream[..., :half_width]
    trailing = upstream[..., half_width:]
    return jnp.concatenate(
        [
            leading * cosine_table + trailing * sine_table,
            trailing * cosine_table - leading * sine_table,
        ],
        -1,
    )


def project(left, right):
    return jnp.dot(left, right, preferred_element_type=jnp.float32)


def against_rows(left, right):
    return lax.dot_general(
        left, right, (((1,), (1,)), ((), ())), preferred_element_type=jnp.float32
    )


def over_tokens(left, right):
    return lax.dot_general(
        left, right, (((0,), (0,)), ((), ())), preferred_element_type=jnp.float32
    )


def split_columns(packed, widths):
    pieces = []
    column_at = 0
    for width_one in widths:
        pieces.append(packed[:, column_at : column_at + width_one])
        column_at = column_at + width_one
    return pieces


def local(
    tokens,
    layer_inputs,
    cotangent,
    doc_lengths,
    w_query,
    w_key,
    w_value,
    w_output,
    laurel_left,
    laurel_right,
    w_gate,
    w_up,
    w_down,
    w_plgate,
    w_plproj,
    g_input,
    g_query,
    g_key,
    g_attn,
    g_laurel,
    g_preffw,
    g_ffw,
    g_perlayer,
):
    gathered = (
        lax.all_gather(w_query, ("batch", "seq", "fsdp"), axis=0, tiled=True),
        lax.all_gather(w_key, ("batch", "seq", "fsdp"), axis=0, tiled=True),
        lax.all_gather(w_value, ("batch", "seq", "fsdp"), axis=0, tiled=True),
        lax.all_gather(w_output, ("batch", "seq", "fsdp"), axis=0, tiled=True),
        lax.all_gather(laurel_left, ("batch", "seq", "fsdp"), axis=0, tiled=True),
        lax.all_gather(laurel_right, ("batch", "seq", "fsdp"), axis=0, tiled=True),
        lax.all_gather(w_gate, ("batch", "seq", "fsdp"), axis=0, tiled=True),
        lax.all_gather(w_up, ("batch", "seq", "fsdp"), axis=0, tiled=True),
        lax.all_gather(w_down, ("batch", "seq", "fsdp"), axis=0, tiled=True),
        lax.all_gather(w_plgate, ("batch", "seq", "fsdp"), axis=0, tiled=True),
        lax.all_gather(w_plproj, ("batch", "seq", "fsdp"), axis=0, tiled=True),
        lax.all_gather(g_input, ("batch", "seq", "fsdp"), axis=0, tiled=True),
        lax.all_gather(g_query, ("batch", "seq", "fsdp"), axis=0, tiled=True),
        lax.all_gather(g_key, ("batch", "seq", "fsdp"), axis=0, tiled=True),
        lax.all_gather(g_attn, ("batch", "seq", "fsdp"), axis=0, tiled=True),
        lax.all_gather(g_laurel, ("batch", "seq", "fsdp"), axis=0, tiled=True),
        lax.all_gather(g_preffw, ("batch", "seq", "fsdp"), axis=0, tiled=True),
        lax.all_gather(g_ffw, ("batch", "seq", "fsdp"), axis=0, tiled=True),
        lax.all_gather(g_perlayer, ("batch", "seq", "fsdp"), axis=0, tiled=True),
    )
    query_w, key_w, value_w, output_w, left_w, right_w, gate_w, up_w, down_w, plgate_w, plproj_w = (
        gathered[:11]
    )
    input_g, query_g, key_g, attn_g, laurel_g, preffw_g, ffw_g, perlayer_g = [
        entry.astype(jnp.float32) for entry in gathered[11:]
    ]
    head_dim = query_g.shape[0]
    num_heads = query_w.shape[1] // head_dim
    kv_heads = key_w.shape[1] // head_dim
    groups = num_heads // kv_heads
    width_kv = kv_heads * head_dim
    score_scale = head_dim ** (-0.5)
    seq_pos = lax.axis_index("seq")
    tok_rows = tokens.shape[1]
    reach_hops = min((WINDOW - 2) // tok_rows + 1, lax.axis_size("seq") - 1)
    resid_in = tokens[0].astype(jnp.float32)
    perlayer = layer_inputs[0].astype(jnp.float32)
    upstream = cotangent[0].astype(jnp.float32)
    lengths = doc_lengths[0]
    places = seq_pos * tok_rows + jnp.arange(tok_rows, dtype=jnp.int32)
    segment, rel_pos = positions_of(places, lengths)
    cosine_table, sine_table = rope_tables(rel_pos, head_dim)
    ff_width = gate_w.shape[1]
    x_normed = rms_norm(resid_in, input_g)
    x_low = x_normed.astype(jnp.bfloat16)
    query_heads = project(x_low, query_w).reshape(tok_rows, num_heads, head_dim)
    key_heads = project(x_low, key_w).reshape(tok_rows, kv_heads, head_dim)
    value_raw = project(x_low, value_w)
    query_low = rotate(rms_norm(query_heads, query_g), cosine_table, sine_table).astype(
        jnp.bfloat16
    )
    key_rot = rotate(rms_norm(key_heads, key_g), cosine_table, sine_table)
    kv_local = jnp.concatenate([key_rot.reshape(tok_rows, width_kv), value_raw], 1).astype(
        jnp.bfloat16
    )
    pieces = []
    for distance in range(reach_hops, 0, -1):
        pieces.append(shifted(kv_local, "seq", distance))
    kv_window = jnp.concatenate(pieces + [kv_local], 0)
    key_places = (seq_pos - reach_hops) * tok_rows + jnp.arange(
        (reach_hops + 1) * tok_rows, dtype=jnp.int32
    )
    key_segment, key_rel = positions_of(key_places, lengths)
    distance_all = places[:, None] - key_places[None, :]
    allowed = (
        (segment[:, None] == key_segment[None, :])
        & (distance_all >= 0)
        & (distance_all < WINDOW)
        & (key_places[None, :] >= 0)
    )
    keys_win = kv_window[:, :width_kv].reshape(-1, kv_heads, head_dim)
    values_win = kv_window[:, width_kv:].reshape(-1, kv_heads, head_dim)
    query_group = query_low.reshape(tok_rows, kv_heads, groups, head_dim)

    def scores_of():
        raw_scores = (
            jnp.einsum("tkgd,skd->kgts", query_group, keys_win, preferred_element_type=jnp.float32)
            * score_scale
        )
        return jnp.where(allowed, raw_scores, -1e30)

    scores = scores_of()
    row_max = jnp.max(scores, -1, keepdims=True)
    row_total = jnp.sum(jnp.exp(scores - row_max), -1, keepdims=True)
    log_total = row_max + jnp.log(row_total)
    attn_probs = jnp.exp(scores - log_total)
    attn_heads = jnp.einsum(
        "kgts,skd->tkgd",
        attn_probs.astype(jnp.bfloat16),
        values_win,
        preferred_element_type=jnp.float32,
    )
    attn_low = attn_heads.reshape(tok_rows, num_heads * head_dim).astype(jnp.bfloat16)
    attn_proj = against_rows(attn_low, output_w)
    left_low = project(x_low, left_w).astype(jnp.bfloat16)
    right_out = against_rows(left_low, right_w)
    hidden = (
        resid_in + rms_norm(attn_proj, attn_g) + x_normed + rms_norm(right_out, laurel_g)
    ) * ROOT_HALF
    ffw_in = rms_norm(hidden, preffw_g).astype(jnp.bfloat16)
    gate_used, up_used, down_used = (gate_w, up_w, down_w)
    gate_out = project(ffw_in, gate_used)
    up_out = project(ffw_in, up_used)
    act_low = geglu(gate_out, up_out).astype(jnp.bfloat16)
    down_terms = against_rows(act_low, down_used)
    second = hidden + rms_norm(down_terms, ffw_g)
    second_low = second.astype(jnp.bfloat16)
    plgate_out = project(second_low, plgate_w)
    gated_low = geglu(plgate_out, perlayer).astype(jnp.bfloat16)
    plproj_out = against_rows(gated_low, plproj_w)
    mixed_out = (second + rms_norm(plproj_out, perlayer_g)).astype(jnp.bfloat16)
    d_plproj, d_perlayer_g = norm_back(plproj_out, perlayer_g, upstream)
    d_plproj_low = d_plproj.astype(jnp.bfloat16)
    d_gated = project(d_plproj_low, plproj_w)
    d_plgate_low = jax.vjp(geglu, plgate_out, perlayer)[1](d_gated)[0].astype(jnp.bfloat16)
    d_second = upstream + against_rows(d_plgate_low, plgate_w)
    d_down, d_ffw_g = norm_back(down_terms, ffw_g, d_second)
    d_down_low = d_down.astype(jnp.bfloat16)
    d_act = project(d_down_low, down_used)
    d_gate, d_up = jax.vjp(geglu, gate_out, up_out)[1](d_act)
    d_gate_low = d_gate.astype(jnp.bfloat16)
    d_up_low = d_up.astype(jnp.bfloat16)
    d_ffw_terms = against_rows(d_gate_low, gate_used) + against_rows(d_up_low, up_used)
    d_hidden_norm, d_preffw_g = norm_back(hidden, preffw_g, d_ffw_terms)
    d_branch = (d_second + d_hidden_norm) * ROOT_HALF
    ffn_grads = lax.psum_scatter(
        jnp.concatenate(
            [
                over_tokens(ffw_in, d_gate_low),
                over_tokens(ffw_in, d_up_low),
                over_tokens(d_down_low, act_low),
            ],
            1,
        ),
        ("batch", "seq", "fsdp"),
        scatter_dimension=0,
        tiled=True,
    )
    d_laurel, d_laurel_g = norm_back(right_out, laurel_g, d_branch)
    d_laurel_low = d_laurel.astype(jnp.bfloat16)
    d_left_low = project(d_laurel_low, right_w).astype(jnp.bfloat16)
    d_attn, d_attn_g = norm_back(attn_proj, attn_g, d_branch)
    d_attn_low = d_attn.astype(jnp.bfloat16)
    d_heads = project(d_attn_low, output_w).astype(jnp.bfloat16)
    d_group = d_heads.reshape(tok_rows, kv_heads, groups, head_dim)
    scores = scores_of()
    attn_probs = jnp.exp(scores - log_total)
    d_probs = jnp.einsum("tkgd,skd->kgts", d_group, values_win, preferred_element_type=jnp.float32)
    d_scores = (attn_probs * (d_probs - jnp.sum(attn_probs * d_probs, -1, keepdims=True))).astype(
        jnp.bfloat16
    )
    d_query_rot = (
        jnp.einsum("kgts,skd->tkgd", d_scores, keys_win, preferred_element_type=jnp.float32)
        * score_scale
    )
    d_keys = (
        jnp.einsum("kgts,tkgd->skd", d_scores, query_group, preferred_element_type=jnp.float32)
        * score_scale
    )
    d_values = jnp.einsum(
        "kgts,tkgd->skd",
        attn_probs.astype(jnp.bfloat16),
        d_group,
        preferred_element_type=jnp.float32,
    )
    d_kv = jnp.concatenate([d_keys.reshape(-1, width_kv), d_values.reshape(-1, width_kv)], 1)
    d_kv_local = d_kv[reach_hops * tok_rows :]
    for distance in range(reach_hops, 0, -1):
        piece_grad = d_kv[
            (reach_hops - distance) * tok_rows : (reach_hops - distance + 1) * tok_rows
        ]
        d_kv_local = d_kv_local + shifted(piece_grad.astype(jnp.bfloat16), "seq", -distance).astype(
            piece_grad.dtype
        )
    d_key_rot = d_kv_local[:, :width_kv].reshape(tok_rows, kv_heads, head_dim)
    d_value_low = d_kv_local[:, width_kv:].astype(jnp.bfloat16)
    d_query_norm = rotate_back(
        d_query_rot.reshape(tok_rows, num_heads, head_dim), cosine_table, sine_table
    )
    d_query_raw, d_query_g = norm_back(query_heads, query_g, d_query_norm)
    d_key_norm = rotate_back(d_key_rot, cosine_table, sine_table)
    d_key_raw, d_key_g = norm_back(key_heads, key_g, d_key_norm)
    d_query_low = d_query_raw.reshape(tok_rows, num_heads * head_dim).astype(jnp.bfloat16)
    d_key_low = d_key_raw.reshape(tok_rows, width_kv).astype(jnp.bfloat16)
    d_x_low = (
        against_rows(d_query_low, query_w)
        + against_rows(d_key_low, key_w)
        + against_rows(d_value_low, value_w)
        + against_rows(d_left_low, left_w)
    )
    d_input, d_input_g = norm_back(resid_in, input_g, d_x_low + d_branch)
    grad_tokens = (d_input + d_branch)[None]
    other_grads = lax.psum_scatter(
        jnp.concatenate(
            [
                over_tokens(x_low, d_query_low),
                over_tokens(x_low, d_key_low),
                over_tokens(x_low, d_value_low),
                over_tokens(d_attn_low, attn_low),
                over_tokens(x_low, d_left_low),
                over_tokens(d_laurel_low, left_low),
                over_tokens(second_low, d_plgate_low),
                over_tokens(d_plproj_low, gated_low),
            ],
            1,
        ),
        ("batch", "seq", "fsdp"),
        scatter_dimension=0,
        tiled=True,
    )
    other_widths = [
        query_w.shape[1],
        key_w.shape[1],
        value_w.shape[1],
        output_w.shape[1],
        left_w.shape[1],
        right_w.shape[1],
        plgate_w.shape[1],
        plproj_w.shape[1],
    ]
    (
        grad_query,
        grad_key,
        grad_value,
        grad_output,
        grad_left,
        grad_right,
        grad_plgate,
        grad_plproj,
    ) = split_columns(other_grads, other_widths)
    grad_gate, grad_up, grad_down = split_columns(ffn_grads, [ff_width, ff_width, ff_width])
    (
        grad_g_input,
        grad_g_query,
        grad_g_key,
        grad_g_attn,
        grad_g_laurel,
        grad_g_preffw,
        grad_g_ffw,
        grad_g_perlayer,
    ) = (
        lax.psum_scatter(d_input_g, ("batch", "seq", "fsdp"), scatter_dimension=0, tiled=True),
        lax.psum_scatter(d_query_g, ("batch", "seq", "fsdp"), scatter_dimension=0, tiled=True),
        lax.psum_scatter(d_key_g, ("batch", "seq", "fsdp"), scatter_dimension=0, tiled=True),
        lax.psum_scatter(d_attn_g, ("batch", "seq", "fsdp"), scatter_dimension=0, tiled=True),
        lax.psum_scatter(d_laurel_g, ("batch", "seq", "fsdp"), scatter_dimension=0, tiled=True),
        lax.psum_scatter(d_preffw_g, ("batch", "seq", "fsdp"), scatter_dimension=0, tiled=True),
        lax.psum_scatter(d_ffw_g, ("batch", "seq", "fsdp"), scatter_dimension=0, tiled=True),
        lax.psum_scatter(d_perlayer_g, ("batch", "seq", "fsdp"), scatter_dimension=0, tiled=True),
    )
    return (
        mixed_out[None],
        grad_tokens,
        grad_query,
        grad_key,
        grad_value,
        grad_output,
        grad_left,
        grad_right,
        grad_gate,
        grad_up,
        grad_down,
        grad_plgate,
        grad_plproj,
        grad_g_input,
        grad_g_query,
        grad_g_key,
        grad_g_attn,
        grad_g_laurel,
        grad_g_preffw,
        grad_g_ffw,
        grad_g_perlayer,
    )


def solution(mesh):
    placed = (
        P(("batch", "fsdp"), "seq", None),
        P(("batch", "fsdp"), "seq", None),
        P(("batch", "fsdp"), "seq", None),
        P(("batch", "fsdp"), None),
        P(("batch", "seq", "fsdp"), None),
        P(("batch", "seq", "fsdp"), None),
        P(("batch", "seq", "fsdp"), None),
        P(("batch", "seq", "fsdp"), None),
        P(("batch", "seq", "fsdp"), None),
        P(("batch", "seq", "fsdp"), None),
        P(("batch", "seq", "fsdp"), None),
        P(("batch", "seq", "fsdp"), None),
        P(("batch", "seq", "fsdp"), None),
        P(("batch", "seq", "fsdp"), None),
        P(("batch", "seq", "fsdp"), None),
        P(("batch", "seq", "fsdp")),
        P(("batch", "seq", "fsdp")),
        P(("batch", "seq", "fsdp")),
        P(("batch", "seq", "fsdp")),
        P(("batch", "seq", "fsdp")),
        P(("batch", "seq", "fsdp")),
        P(("batch", "seq", "fsdp")),
        P(("batch", "seq", "fsdp")),
    )
    return jax.shard_map(
        local,
        mesh=mesh,
        in_specs=placed,
        out_specs=(
            P(("batch", "fsdp"), "seq", None),
            P(("batch", "fsdp"), "seq", None),
            P(("batch", "seq", "fsdp"), None),
            P(("batch", "seq", "fsdp"), None),
            P(("batch", "seq", "fsdp"), None),
            P(("batch", "seq", "fsdp"), None),
            P(("batch", "seq", "fsdp"), None),
            P(("batch", "seq", "fsdp"), None),
            P(("batch", "seq", "fsdp"), None),
            P(("batch", "seq", "fsdp"), None),
            P(("batch", "seq", "fsdp"), None),
            P(("batch", "seq", "fsdp"), None),
            P(("batch", "seq", "fsdp"), None),
            P(("batch", "seq", "fsdp")),
            P(("batch", "seq", "fsdp")),
            P(("batch", "seq", "fsdp")),
            P(("batch", "seq", "fsdp")),
            P(("batch", "seq", "fsdp")),
            P(("batch", "seq", "fsdp")),
            P(("batch", "seq", "fsdp")),
            P(("batch", "seq", "fsdp")),
        ),
        check_vma=False,
    )
```

profile of v0, /device:TPU:0, one launch (start us, length us, event | category | flops | bytes accessed | tf_op | source)
XLA Modules:
  0.0 3281.2 jit_solution(3001191479970373139)
XLA Ops:
  17.9 42.5 %all-reduce.17 = (bf16[2048]{0:T(1024)(128)(2,1)S(1)}, bf16[256]{0:T(256)(128)(2,1)S(1)}, bf16[256]{0:T(256)(128)(2,1)S(1)}, bf16[2048]{0:T(1024)(128)(2,1)S(1)}...) all-reduce(bf16[2048]{0:T(1024)(128)(2,1)S(1)} %dynamic-update-slic, ...), channel_id=1, replica_groups=mesh['batch'=4,'seq'=2,'fsdp'=4] {'batch','seq','fsdp'}, use_global_device_ids=true, to_apply=%add | all-reduce | flops 12800 | bytes 51200
  61.8 71.3 %all_gather.65 = bf16[2048,64]{1,0:T(8,128)(2,1)S(1)} all-gather(bf16[64,64]{1,0:T(8,128)(2,1)S(1)} %copy-done.98), channel_id=1, replica_groups=mesh['batch'=4,'seq'=2,'fsdp'=4] {'batch','seq','fsdp'}, dimensions={0}, use_global_device_ids=true | all-gather | bytes 270336 | tf_op jit(solution)/shard_map/all_gather | solution.py:130
  133.0 71.9 %all_gather.66 = bf16[2048,64]{1,0:T(8,128)(2,1)S(1)} all-gather(bf16[64,64]{1,0:T(8,128)(2,1)S(1)} %copy-done.99), channel_id=1, replica_groups=mesh['batch'=4,'seq'=2,'fsdp'=4] {'batch','seq','fsdp'}, dimensions={0}, use_global_device_ids=true | all-gather | bytes 270336 | tf_op jit(solution)/shard_map/all_gather | solution.py:131
  206.9 3.9 copy.86
  210.8 3.0 multiply_reduce_fusion.18
  216.1 3.0 convolution_convert_fusion.2
  220.9 2.8 multiply_reduce_fusion.13
  227.1 12.3 copy.87
  239.5 7.1 multiply_reduce_fusion.15
  248.7 2.0 subtract_convert_fusion
  250.7 2.3 copy.88
  253.0 2.3 copy.89
  255.3 11.4 fusion.11
  266.7 9.3 exponential_reduce_fusion
  276.0 12.4 convolution_convert_fusion.1
  290.1 8.1 multiply_reduce_fusion.14
  298.8 2.4 multiply_reduce_fusion.12
  303.7 182.6 %all-gather.18.cloned.1.call-done = bf16[2048,8192]{1,0:T(8,128)(2,1)} async-done(((bf16[64,8192]{1,0:T(8,128)(2,1)}), bf16[2048,8192]{1,0:T(8,128)(2,1)}) %all-gather.18.cloned.1.call-update) | async-done | bytes 33554448 | tf_op jit(solution)/shard_map/all_gather | solution.py:132
  486.3 26.6 fusion.98
  512.9 169.2 %all-gather.20.cloned.1.call-done = bf16[2048,8192]{1,0:T(8,128)(2,1)} async-done(((bf16[64,8192]{1,0:T(8,128)(2,1)}), bf16[2048,8192]{1,0:T(8,128)(2,1)}) %all-gather.20.cloned.1.call-update) | async-done | bytes 33554448 | tf_op jit(solution)/shard_map/all_gather | solution.py:133
  682.1 36.3 %multiply_convert_fusion.1 = (bf16[512,8192]{1,0:T(8,128)(2,1)}, f32[512,8192]{1,0:T(8,128)}) fusion(f32[512,8192]{1,0:T(8,128)} %fusion.98, bf16[512,2048]{1,0:T(8,128)(2,1)S(1)} %multiply_convert_fusion.2, bf16[2048,8192]{1,0:T(8,128)(2,1)} %all-gather.20.cloned.1.call-done), kind=kOutput, calls=%fused_computation.17 | convolution fusion | flops 17221812224 | bytes 77594624 | tf_op jit(solution)/shard_map/dot_general | solution.py:76
  718.4 159.6 %all-gather.22.cloned.1.call-done = bf16[2048,8192]{1,0:T(8,128)(2,1)} async-done(((bf16[64,8192]{1,0:T(8,128)(2,1)}), bf16[2048,8192]{1,0:T(8,128)(2,1)}) %all-gather.22.cloned.1.call-update) | async-done | bytes 33554448 | tf_op jit(solution)/shard_map/all_gather | solution.py:134
  878.0 24.3 multiply_reduce_fusion.11
  902.4 2.0 copy-done.15
  904.4 2.7 multiply_add_fusion
  907.1 25.9 all-gather.24.cloned.1.call-done
  932.9 3.2 fusion.55
  936.2 52.5 %all-gather.26.cloned.1.call-done = bf16[2048,256]{1,0:T(8,128)(2,1)} async-done(((bf16[64,256]{1,0:T(8,128)(2,1)}), bf16[2048,256]{1,0:T(8,128)(2,1)}) %all-gather.26.cloned.1.call-update) | async-done | bytes 1048592 | tf_op jit(solution)/shard_map/all_gather | solution.py:136
  988.7 2.1 multiply_reduce_fusion.10
  993.0 3.1 fusion.30
  999.9 2.1 multiply_reduce_fusion
  1004.1 37.2 %multiply_convert_fusion = (bf16[512,8192]{1,0:T(8,128)(2,1)}, bf16[512,8192]{1,0:T(8,128)(2,1)}) fusion(f32[512,8192]{1,0:T(8,128)} %fusion.98, f32[512,8192]{1,0:T(8,128)} %get-tuple-element.163, bf16[512,2048]{1,0:T(8,128)(2,1)S(1)} %fusion.31, bf16[2048,8192]{1,0:T(8,128)(2,1)} %all-gather.22.cloned.1.call-done), kind=kOutput, calls=%fused_computation.16 | convolution fusion | flops 17280532480 | bytes 85983232 | tf_op jit(solution)/shard_map/dot_general | solution.py:76
  1041.3 25.4 fusion.99
  1066.8 27.4 multiply_reduce_fusion.1
  1094.3 8.8 multiply_reduce_fusion.2
  1103.2 2.9 fusion.33
  1107.5 1.9 copy-done.114
  1109.5 5.9 convolution_convert_fusion
  1115.4 2.9 copy.132
  1118.4 8.3 fusion.76
  1126.7 11.9 fusion.7
  1138.6 16.6 fusion.9
  1155.2 6.2 bitcast_multiply_fusion.1
  1161.4 2.3 convolution_multiply_fusion
  1166.0 2.2 multiply_reduce_fusion.4
  1172.6 8.4 convolution_dynamic-update-slice_fusion.1
  1185.3 3.5 convolution_dynamic-update-slice_fusion.3
  1188.7 3.5 convolution_dynamic-update-slice_fusion.2
  1192.2 8.1 convolution_dynamic-update-slice_fusion
  1203.2 2.1 convolution_dynamic-update-slice_fusion.5
  1205.3 2.2 convolution_dynamic-update-slice_fusion.4
  1207.5 45.9 %copy.122 = f32[2048,5760]{1,0:T(8,128)} copy(f32[2048,5760]{0,1:T(8,128)} %convolution_dynamic-update-slice_fusion.4) | data formatting | bytes 94371840
  1253.4 44.7 %fusion.105 = f32[2048,8192]{1,0:T(8,128)} fusion(bf16[512,2048]{1,0:T(8,128)(2,1)} %copy-done.30, bf16[512,8192]{1,0:T(8,128)(2,1)} %get-tuple-element.162), kind=kOutput, calls=%fused_computation.212 | convolution fusion | flops 17179869184 | bytes 77594624 | tf_op jit(solution)/shard_map/dot_general | solution.py:86
  1298.2 35.6 %fusion.104 = f32[2048,8192]{1,0:T(8,128)} fusion(bf16[512,2048]{1,0:T(8,128)(2,1)S(1)} %copy-done.19, bf16[512,8192]{1,0:T(8,128)(2,1)} %get-tuple-element.121), kind=kOutput, calls=%fused_computation.211 | convolution fusion | flops 17179869184 | bytes 77594624 | tf_op jit(solution)/shard_map/dot_general | solution.py:86
  1333.8 30.3 fusion.103
  1364.1 133.7 %pad_maximum_fusion = f32[2048,24576]{1,0:T(8,128)} fusion(f32[2048,8192]{1,0:T(8,128)} %fusion.105, f32[2048,8192]{1,0:T(8,128)} %fusion.104, f32[2048,8192]{1,0:T(8,128)} %fusion.103), kind=kLoop, calls=%fused_computation | loop fusion | flops 100663296 | bytes 402653184 | tf_op jit(solution)/shard_map/concatenate | solution.py:252
  1499.8 7.3 fusion.100
  1510.6 5.8 fusion.25
  1516.5 45.3 %all-reduce.16 = (f32[2048]{0:T(1024)S(1)}, f32[256]{0:T(256)S(1)}, f32[256]{0:T(256)S(1)}, f32[2048]{0:T(1024)S(1)}, f32[2048]{0:T(1024)S(1)}, /*index=5*/f32[2...) all-reduce(f32[2048]{0:T(1024)S(1)} %get-tuple-element.96, ...), channel_id=4, replica_groups=mesh['batch'=4,'seq'=2,'fsdp'=4] {'batch','seq','fsdp'}, use_global_device_ids=true, to_apply=%region_26.27.clone | all-reduce | flops 12800 | bytes 102400
  1566.4 6.8 fusion.37
  1573.2 89.7 %reduce-scatter.7.cloned.1.call-done = f32[64,5760]{1,0:T(8,128)} async-done(((f32[2048,5760]{1,0:T(8,128)}), f32[64,5760]{1,0:T(8,128)}) %reduce-scatter.7.cloned.1.call-update) | async-done | bytes 1474576
  1667.6 2.3 fusion.96
  1669.9 1598.5 %reduce-scatter.5.cloned.1.call-done = f32[64,24576]{1,0:T(8,128)} async-done(((f32[2048,24576]{1,0:T(8,128)}), f32[64,24576]{1,0:T(8,128)}) %reduce-scatter.5.cloned.1.call-update) | async-done | bytes 6291472 | tf_op jit(solution)/shard_map/reduce_scatter | solution.py:251
  3268.4 5.7 fusion.92
  (367 shorter events, 65.7 us)
Async XLA Ops:
  7.2 8.9 copy-start.116
  7.2 9.2 copy-start.117
  7.2 9.4 copy-start.118
  7.2 9.7 copy-start.119
  7.3 9.9 copy-start.120
  7.3 10.2 copy-start.121
  7.3 10.4 copy-start.122
  7.3 54.5 %copy-start.98 = (bf16[64,64]{1,0:T(8,128)(2,1)S(1)}, bf16[64,64]{1,0:T(8,128)(2,1)}, u32[]{:S(2)}) copy-start(bf16[64,64]{1,0:T(8,128)(2,1)} %param.31) | copy-start | bytes 24580
  7.3 125.7 %copy-start.99 = (bf16[64,64]{1,0:T(8,128)(2,1)S(1)}, bf16[64,64]{1,0:T(8,128)(2,1)}, u32[]{:S(2)}) copy-start(bf16[64,64]{1,0:T(8,128)(2,1)} %param.32) | copy-start | bytes 24580
  7.3 199.6 %all-gather.10.cloned.1.call-start = ((), (), s32[]{:S(2)}) async-start(), calls=%async_computation.2 | async-start | bytes 2162688 | tf_op jit(solution)/shard_map/all_gather | solution.py:127
  8.0 208.0 %all-gather.12.cloned.1.call-start = ((), (), s32[]{:S(2)}) async-start(), calls=%async_computation.3 | async-start | bytes 2162688 | tf_op jit(solution)/shard_map/all_gather | solution.py:128
  8.8 218.3 %all-gather.14.cloned.1.call-start = ((), (), s32[]{:S(2)}) async-start(), calls=%async_computation.4 | async-start | bytes 8650752 | tf_op jit(solution)/shard_map/all_gather | solution.py:126
  9.5 280.6 %all-gather.16.cloned.1.call-start = ((), (), s32[]{:S(2)}) async-start(), calls=%async_computation.5 | async-start | bytes 8650752 | tf_op jit(solution)/shard_map/all_gather | solution.py:129
  10.1 476.2 %all-gather.18.cloned.1.call-start = ((), (), s32[]{:S(2)}) async-start(), calls=%async_computation.6 | async-start | bytes 34603008 | tf_op jit(solution)/shard_map/all_gather | solution.py:132
  10.7 671.4 %all-gather.20.cloned.1.call-start = ((), (), s32[]{:S(2)}) async-start(), calls=%async_computation.7 | async-start | bytes 34603008 | tf_op jit(solution)/shard_map/all_gather | solution.py:133
  11.3 866.7 %all-gather.22.cloned.1.call-start = ((), (), s32[]{:S(2)}) async-start(), calls=%async_computation.8 | async-start | bytes 34603008 | tf_op jit(solution)/shard_map/all_gather | solution.py:134
  12.0 920.9 %all-gather.24.cloned.1.call-start = ((), (), s32[]{:S(2)}) async-start(), calls=%async_computation.9 | async-start | bytes 1081344 | tf_op jit(solution)/shard_map/all_gather | solution.py:135
  12.8 975.9 %all-gather.26.cloned.1.call-start = ((), (), s32[]{:S(2)}) async-start(), calls=%async_computation.10 | async-start | bytes 1081344 | tf_op jit(solution)/shard_map/all_gather | solution.py:136
  13.5 1649.4 %reduce-scatter.7.cloned.1.call-start = ((), (), s32[]{:S(2)}) async-start(), calls=%async_computation.12 | async-start | bytes 48660480
  15.6 46.2 %copy-start.94 = (f32[512]{0:T(512)}, f32[512]{0:T(512)S(1)}, u32[]{:S(2)}) copy-start(f32[512]{0:T(512)S(1)} %fusion.26) | copy-start | bytes 6148
  15.6 283.2 %copy-start.81 = (f32[512]{0:T(512)}, f32[512]{0:T(512)S(1)}, u32[]{:S(2)}) copy-start(f32[512]{0:T(512)S(1)} %fusion.67) | copy-start | bytes 6148
  60.5 153.4 %copy-start.102 = (f32[256]{0:T(256)}, f32[256]{0:T(256)S(1)}, u32[]{:S(2)}) copy-start(f32[256]{0:T(256)S(1)} %convert_element_type.161) | copy-start | bytes 3076
  60.5 186.2 %copy-start.104 = (f32[256]{0:T(256)}, f32[256]{0:T(256)S(1)}, u32[]{:S(2)}) copy-start(f32[256]{0:T(256)S(1)} %convert_element_type.166) | copy-start | bytes 3076
  60.5 238.3 %copy-start.66 = (f32[2048]{0:T(1024)}, f32[2048]{0:T(1024)S(1)}, u32[]{:S(2)}) copy-start(f32[2048]{0:T(1024)S(1)} %convert_element_type.158) | copy-start | bytes 24580
  60.5 241.4 %copy-start.74 = (f32[2048]{0:T(1024)}, f32[2048]{0:T(1024)S(1)}, u32[]{:S(2)}) copy-start(f32[2048]{0:T(1024)S(1)} %convert_element_type.174) | copy-start | bytes 24580
  133.0 72.9 %copy-start.48 = (bf16[2048,64]{1,0:T(8,128)(2,1)}, bf16[2048,64]{1,0:T(8,128)(2,1)S(1)}, u32[]{:S(2)}) copy-start(bf16[2048,64]{1,0:T(8,128)(2,1)S(1)} %all_gather.65) | copy-start | bytes 786436
  205.0 15.9 copy-start.37
  206.0 41.5 %copy-start.33 = (f32[512,128]{0,1:T(8,128)}, f32[512,128]{0,1:T(8,128)S(1)}, u32[]{:S(2)}) copy-start(f32[512,128]{0,1:T(8,128)S(1)} %get-tuple-element.148) | copy-start | bytes 786436
  206.0 41.5 %copy-start.35 = (f32[512,128]{0,1:T(8,128)}, f32[512,128]{0,1:T(8,128)S(1)}, u32[]{:S(2)}) copy-start(f32[512,128]{0,1:T(8,128)S(1)} %get-tuple-element.149) | copy-start | bytes 786436
  206.8 14.1 copy-start.62
  219.2 6.1 collective-permute-start
  223.7 75.1 %copy-start.84 = (f32[512]{0:T(512)}, f32[512]{0:T(512)S(1)}, u32[]{:S(2)}) copy-start(f32[512]{0:T(512)S(1)} %fusion.69) | copy-start | bytes 6148
  225.3 50.8 %copy-start.22 = (pred[512,1024]{0,1:T(8,128)(4,1)}, pred[512,1024]{0,1:T(8,128)(4,1)S(1)}, u32[]{:S(2)}) copy-start(pred[512,1024]{0,1:T(8,128)(4,1)S(1)} %fusion.51) | copy-start | bytes 1572868
  276.0 12.4 copy-start.69
  301.3 211.6 %copy-start.92 = (f32[512]{0:T(512)}, f32[512]{0:T(512)S(1)}, u32[]{:S(2)}) copy-start(f32[512]{0:T(512)S(1)} %get-tuple-element.119) | copy-start | bytes 6148
  301.9 211.0 %copy-start.107 = (f32[512]{0:T(512)}, f32[512]{0:T(512)S(1)}, u32[]{:S(2)}) copy-start(f32[512]{0:T(512)S(1)} %get-tuple-element.151) | copy-start | bytes 6148
  303.7 378.4 %copy-start.18 = (bf16[512,2048]{1,0:T(8,128)(2,1)}, bf16[512,2048]{1,0:T(8,128)(2,1)S(1)}, u32[]{:S(2)}) copy-start(bf16[512,2048]{1,0:T(8,128)(2,1)S(1)} %multiply_convert_fusion.2) | copy-start | bytes 6291460
  878.0 26.4 copy-start.3
  878.0 26.4 copy-start.71
  907.1 81.6 %copy-start.52 = (bf16[1,512,256]{2,1,0:T(8,128)(2,1)S(1)}, bf16[1,512,256]{2,1,0:T(8,128)(2,1)}, u32[]{:S(2)}) copy-start(bf16[1,512,256]{2,1,0:T(8,128)(2,1)} %param.24) | copy-start | bytes 786436
  936.1 59.9 %copy-start.40 = (f32[512,256]{1,0:T(8,128)}, f32[512,256]{1,0:T(8,128)S(1)}, u32[]{:S(2)}) copy-start(f32[512,256]{1,0:T(8,128)S(1)} %fusion.55) | copy-start | bytes 1572868
  936.2 54.7 %copy-start.21 = (bf16[1,512,2048]{2,1,0:T(8,128)(2,1)S(1)}, bf16[1,512,2048]{2,1,0:T(8,128)(2,1)}, u32[]{:S(2)}) copy-start(bf16[1,512,2048]{2,1,0:T(8,128)(2,1)} %param.25) | copy-start | bytes 6291460
  936.2 54.7 %copy-start.76 = (f32[2048]{0:T(1024)S(1)}, f32[2048]{0:T(1024)}, u32[]{:S(2)}) copy-start(f32[2048]{0:T(1024)} %convert_element_type.182) | copy-start | bytes 24580
  1004.1 37.2 %copy-start.30 = (bf16[512,2048]{1,0:T(8,128)(2,1)}, bf16[512,2048]{1,0:T(8,128)(2,1)S(1)}, u32[]{:S(2)}) copy-start(bf16[512,2048]{1,0:T(8,128)(2,1)S(1)} %fusion.31) | copy-start | bytes 6291460
  1041.3 25.4 copy-start.75
  1041.3 25.4 copy-start.108
  1066.8 27.5 copy-start.93
  1066.8 27.5 copy-start.1
  1066.8 27.5 copy-start.72
  1066.8 27.5 copy-start.73
  1066.8 27.5 copy-start.85
  1066.8 27.5 copy-start.87
  1066.8 27.5 copy-start.106
  1094.3 8.8 copy-start.97
  1094.3 8.8 copy-start.14
  1138.6 16.6 copy-start.56
  1138.6 16.6 copy-start.57
  1169.4 11.7 copy-start.50
  1169.6 11.4 collective-permute-start.1
  1172.6 27.7 copy-start.64
  1192.2 9.7 copy-start.63
  1253.4 44.8 %copy-start.19 = (bf16[512,2048]{1,0:T(8,128)(2,1)S(1)}, bf16[512,2048]{1,0:T(8,128)(2,1)}, u32[]{:S(2)}) copy-start(bf16[512,2048]{1,0:T(8,128)(2,1)} %copy-done.18) | copy-start | bytes 6291460
  1253.4 2015.0 %reduce-scatter.5.cloned.1.call-start = ((), (), s32[]{:S(2)}) async-start(), calls=%async_computation.11 | async-start | bytes 207618048 | tf_op jit(solution)/shard_map/reduce_scatter | solution.py:251
  1510.6 55.8 %copy-start.95 = (f32[512]{0:T(512)S(1)}, f32[512]{0:T(512)}, u32[]{:S(2)}) copy-start(f32[512]{0:T(512)} %copy-done.94) | copy-start | bytes 6148
  (73 other events, 255.7 us)
Sparse Core Ops, SparseCore 0:
  11.1 59.3 all-gather.9
  73.4 56.0 all-gather.11
  132.4 78.0 all-gather.13
  213.2 76.8 all-gather.15
  292.9 193.3 all-gather.17
  489.1 192.9 all-gather.19
  685.0 192.9 all-gather.21
  881.0 51.9 all-gather.23
  935.9 52.7 all-gather.25
  1253.5 409.3 reduce-scatter.6
  1670.5 1597.9 reduce-scatter.4
where the time goes:
time: 3290 us; the launch traced here: 3280 us
  waiting for transfers between devices  2290 us (70%)
  matrix products  426 us (13%)
  blocking collectives  231 us (7%)
  other arithmetic  206 us (6%)
  local copies, waits for them, and re-layouts  113 us (3%)
    reduce_scatter x1, waiting for transfers between devices, local(): lax.psum_scatter(jnp.concatenate([over_tokens(ffw_in, d_gate_low), over_t...  1600 us
    all_gather x1, waiting for transfers between devices, local(): lax.all_gather(w_gate, ('batch', 'seq', 'fsdp'), axis=0, tiled=True)  183 us
    all_gather x1, waiting for transfers between devices, local(): lax.all_gather(w_up, ('batch', 'seq', 'fsdp'), axis=0, tiled=True)  169 us
    all_gather x1, waiting for transfers between devices, local(): lax.all_gather(w_down, ('batch', 'seq', 'fsdp'), axis=0, tiled=True)  160 us
    dot_general x11, matrix products, over_tokens(): lax.dot_general(left, right, (((0,), (0,)), ((), ())), preferred_element_...  141 us
    concatenate x1, other arithmetic, local(): jnp.concatenate([over_tokens(ffw_in, d_gate_low), over_tokens(ffw_in, d_u...  134 us
    dot_general x11, matrix products, project(): return jnp.dot(left, right, preferred_element_type=jnp.float32)  125 us
    dot_general x11, matrix products, against_rows(): lax.dot_general(left, right, (((1,), (1,)), ((), ())), preferred_element_...  107 us
  transfers between devices with their start and end apart: 13, of which 8 were waited for; matrix products, arithmetic and copies ran while one was open for 15% of the time, Pallas kernels for 0%

commit v1 on v0

--- a/solution.py
+++ b/solution.py
@@ -4,6 +4,8 @@
 from jax.sharding import PartitionSpec as P
 
 WINDOW = 512
+ALL_AXES = ("batch", "seq", "fsdp")
+ROW_AXES = ("batch", "fsdp")
 
 
 EPS = 1e-06
@@ -97,7 +99,7 @@
     return pieces
 
 
-def local(
+def whole_gather_plan(
     tokens,
     layer_inputs,
     cotangent,
@@ -123,25 +125,25 @@
     g_perlayer,
 ):
     gathered = (
-        lax.all_gather(w_query, ("batch", "seq", "fsdp"), axis=0, tiled=True),
-        lax.all_gather(w_key, ("batch", "seq", "fsdp"), axis=0, tiled=True),
-        lax.all_gather(w_value, ("batch", "seq", "fsdp"), axis=0, tiled=True),
-        lax.all_gather(w_output, ("batch", "seq", "fsdp"), axis=0, tiled=True),
-        lax.all_gather(laurel_left, ("batch", "seq", "fsdp"), axis=0, tiled=True),
-        lax.all_gather(laurel_right, ("batch", "seq", "fsdp"), axis=0, tiled=True),
-        lax.all_gather(w_gate, ("batch", "seq", "fsdp"), axis=0, tiled=True),
-        lax.all_gather(w_up, ("batch", "seq", "fsdp"), axis=0, tiled=True),
-        lax.all_gather(w_down, ("batch", "seq", "fsdp"), axis=0, tiled=True),
-        lax.all_gather(w_plgate, ("batch", "seq", "fsdp"), axis=0, tiled=True),
-        lax.all_gather(w_plproj, ("batch", "seq", "fsdp"), axis=0, tiled=True),
-        lax.all_gather(g_input, ("batch", "seq", "fsdp"), axis=0, tiled=True),
-        lax.all_gather(g_query, ("batch", "seq", "fsdp"), axis=0, tiled=True),
-        lax.all_gather(g_key, ("batch", "seq", "fsdp"), axis=0, tiled=True),
-        lax.all_gather(g_attn, ("batch", "seq", "fsdp"), axis=0, tiled=True),
-        lax.all_gather(g_laurel, ("batch", "seq", "fsdp"), axis=0, tiled=True),
-        lax.all_gather(g_preffw, ("batch", "seq", "fsdp"), axis=0, tiled=True),
-        lax.all_gather(g_ffw, ("batch", "seq", "fsdp"), axis=0, tiled=True),
-        lax.all_gather(g_perlayer, ("batch", "seq", "fsdp"), axis=0, tiled=True),
+        lax.all_gather(w_query, ALL_AXES, axis=0, tiled=True),
+        lax.all_gather(w_key, ALL_AXES, axis=0, tiled=True),
+        lax.all_gather(w_value, ALL_AXES, axis=0, tiled=True),
+        lax.all_gather(w_output, ALL_AXES, axis=0, tiled=True),
+        lax.all_gather(laurel_left, ALL_AXES, axis=0, tiled=True),
+        lax.all_gather(laurel_right, ALL_AXES, axis=0, tiled=True),
+        lax.all_gather(w_gate, ALL_AXES, axis=0, tiled=True),
+        lax.all_gather(w_up, ALL_AXES, axis=0, tiled=True),
+        lax.all_gather(w_down, ALL_AXES, axis=0, tiled=True),
+        lax.all_gather(w_plgate, ALL_AXES, axis=0, tiled=True),
+        lax.all_gather(w_plproj, ALL_AXES, axis=0, tiled=True),
+        lax.all_gather(g_input, ALL_AXES, axis=0, tiled=True),
+        lax.all_gather(g_query, ALL_AXES, axis=0, tiled=True),
+        lax.all_gather(g_key, ALL_AXES, axis=0, tiled=True),
+        lax.all_gather(g_attn, ALL_AXES, axis=0, tiled=True),
+        lax.all_gather(g_laurel, ALL_AXES, axis=0, tiled=True),
+        lax.all_gather(g_preffw, ALL_AXES, axis=0, tiled=True),
+        lax.all_gather(g_ffw, ALL_AXES, axis=0, tiled=True),
+        lax.all_gather(g_perlayer, ALL_AXES, axis=0, tiled=True),
     )
     query_w, key_w, value_w, output_w, left_w, right_w, gate_w, up_w, down_w, plgate_w, plproj_w = (
         gathered[:11]
@@ -257,7 +259,7 @@
             ],
             1,
         ),
-        ("batch", "seq", "fsdp"),
+        ALL_AXES,
         scatter_dimension=0,
         tiled=True,
     )
@@ -329,7 +331,7 @@
             ],
             1,
         ),
-        ("batch", "seq", "fsdp"),
+        ALL_AXES,
         scatter_dimension=0,
         tiled=True,
     )
@@ -364,14 +366,14 @@
         grad_g_ffw,
         grad_g_perlayer,
     ) = (
-        lax.psum_scatter(d_input_g, ("batch", "seq", "fsdp"), scatter_dimension=0, tiled=True),
-        lax.psum_scatter(d_query_g, ("batch", "seq", "fsdp"), scatter_dimension=0, tiled=True),
-        lax.psum_scatter(d_key_g, ("batch", "seq", "fsdp"), scatter_dimension=0, tiled=True),
-        lax.psum_scatter(d_attn_g, ("batch", "seq", "fsdp"), scatter_dimension=0, tiled=True),
-        lax.psum_scatter(d_laurel_g, ("batch", "seq", "fsdp"), scatter_dimension=0, tiled=True),
-        lax.psum_scatter(d_preffw_g, ("batch", "seq", "fsdp"), scatter_dimension=0, tiled=True),
-        lax.psum_scatter(d_ffw_g, ("batch", "seq", "fsdp"), scatter_dimension=0, tiled=True),
-        lax.psum_scatter(d_perlayer_g, ("batch", "seq", "fsdp"), scatter_dimension=0, tiled=True),
+        lax.psum_scatter(d_input_g, ALL_AXES, scatter_dimension=0, tiled=True),
+        lax.psum_scatter(d_query_g, ALL_AXES, scatter_dimension=0, tiled=True),
+        lax.psum_scatter(d_key_g, ALL_AXES, scatter_dimension=0, tiled=True),
+        lax.psum_scatter(d_attn_g, ALL_AXES, scatter_dimension=0, tiled=True),
+        lax.psum_scatter(d_laurel_g, ALL_AXES, scatter_dimension=0, tiled=True),
+        lax.psum_scatter(d_preffw_g, ALL_AXES, scatter_dimension=0, tiled=True),
+        lax.psum_scatter(d_ffw_g, ALL_AXES, scatter_dimension=0, tiled=True),
+        lax.psum_scatter(d_perlayer_g, ALL_AXES, scatter_dimension=0, tiled=True),
     )
     return (
         mixed_out[None],
@@ -398,58 +400,656 @@
     )
 
 
+BF16 = jnp.bfloat16
+X_PAIRS = [(0, 1), (1, 0), (2, 3), (3, 2)]
+Y_PAIRS = [(0, 2), (2, 0), (1, 3), (3, 1)]
+CORE_PAIRS = [(0, 1), (1, 0)]
+
+
+def swap_x(array):
+    return lax.ppermute(array, "batch", X_PAIRS)
+
+
+def swap_y(array):
+    return lax.ppermute(array, "batch", Y_PAIRS)
+
+
+def swap_core(array):
+    return lax.ppermute(array, "seq", CORE_PAIRS)
+
+
+def chained(swap, pieces, earlier=()):
+    there = list(earlier)
+    for piece in pieces:
+        there.append(swap(after(piece, there[-2]) if len(there) > 1 else piece))
+    return there[len(earlier) :]
+
+
+def pick(array, axis, index):
+    return lax.dynamic_index_in_dim(array, index, axis, keepdims=False)
+
+
+def in_order(index, mine, theirs, axis):
+    first = jnp.where(index == 0, mine, theirs)
+    second = jnp.where(index == 0, theirs, mine)
+    return jnp.stack([first, second], axis)
+
+
+def halves_by(index, array, axis):
+    low, high = jnp.split(array, 2, axis)
+    return jnp.concatenate(
+        [jnp.where(index == 0, low, high), jnp.where(index == 0, high, low)], axis
+    )
+
+
+def to_pairs(x_at, array, axis):
+    b0, b1, b2, b3 = jnp.split(array, 4, axis)
+    even = x_at == 0
+    return jnp.concatenate(
+        [
+            jnp.where(even, b0, b1),
+            jnp.where(even, b2, b3),
+            jnp.where(even, b1, b0),
+            jnp.where(even, b3, b2),
+        ],
+        axis,
+    )
+
+
+def from_pairs(x_at, array, axis):
+    e0, e1, e2, e3 = jnp.split(array, 4, axis)
+    even = x_at == 0
+    return jnp.concatenate(
+        [
+            jnp.where(even, e0, e2),
+            jnp.where(even, e2, e0),
+            jnp.where(even, e1, e3),
+            jnp.where(even, e3, e1),
+        ],
+        axis,
+    )
+
+
+def after(array, earlier):
+    return lax.optimization_barrier((array, earlier))[0]
+
+
+def gather_z(array):
+    kinds, rows, width = array.shape
+    stacked = lax.all_gather(array, "fsdp", axis=0, tiled=False)
+    return [stacked[:, kind].reshape(-1, width) for kind in range(kinds)]
+
+
+def scatter_z(ordered):
+    count, kinds, rows, width = ordered.shape
+    flat = ordered.reshape(count * kinds * rows, width)
+    return lax.psum_scatter(flat, "fsdp", scatter_dimension=0, tiled=True)
+
+
+def scatter_z_small(ordered):
+    count = lax.axis_size("fsdp")
+    z_at = lax.axis_index("fsdp")
+    total = pick(ordered, 0, z_at).astype(jnp.float32)
+    for by in range(1, count):
+        turn = [(i, (i + by) % count) for i in range(count)]
+        sent = pick(ordered, 0, lax.rem(z_at + by, count))
+        total = total + lax.ppermute(sent, "fsdp", turn).astype(jnp.float32)
+    return total.astype(BF16)
+
+
+def sum_all(array):
+    array = array + swap_core(array)
+    array = array + swap_x(array)
+    array = array + swap_y(array)
+    count = lax.axis_size("fsdp")
+    turns = [
+        lax.ppermute(array, "fsdp", [(i, (i + by) % count) for i in range(count)])
+        for by in range(1, count)
+    ]
+    return sum(turns, array)
+
+
+def gate_up_act(left, gate_w, up_w):
+    gate, up = project(left, gate_w), project(left, up_w)
+    return gate.astype(BF16), up.astype(BF16), geglu(gate, up).astype(BF16)
+
+
+def gate_up_back(left, down_w, gate, up):
+    gate, up = gate.astype(jnp.float32), up.astype(jnp.float32)
+    d_gate, d_up = jax.vjp(geglu, gate, up)[1](project(left, down_w))
+    return d_gate.astype(BF16), d_up.astype(BF16)
+
+
+def onto_model(lefts, weights):
+    half = lefts[0].shape[0] // 2
+
+    def total(cut):
+        terms = [against_rows(left[cut], weight) for left, weight in zip(lefts, weights)]
+        return sum(terms[1:], terms[0])
+
+    return total(slice(0, half)), total(slice(half, None)).astype(BF16)
+
+
+def weight_sum(sides, start, length, split, received=(), ordered=False):
+    kinds, places, rows = split
+    parts = []
+    for part in range(len(sides[0][1])):
+        total = None
+        for left, rights in sides:
+            array, at, width = rights[part]
+            term = over_tokens(left[:, start : start + length], array[:, at : at + width])
+            total = term if total is None else total + term
+        parts.append(total)
+    groups = [group if isinstance(group, tuple) else (group,) for group in received]
+    for pieces in zip(*groups):
+        whole, at = jnp.concatenate(pieces, 0), 0
+        for number, total in enumerate(parts):
+            width = total.shape[1]
+            parts[number] = total + whole[:, at : at + width].astype(jnp.float32)
+            at += width
+    whole = [total.astype(BF16) for total in parts]
+    whole = jnp.concatenate(whole, 1) if len(whole) > 1 else whole[0]
+    if not ordered:
+        return jnp.split(whole, length // (places * rows), 0)
+    cut = whole.reshape(length // (places * rows), places, rows, whole.shape[1])
+    return jnp.transpose(cut, (1, 0, 2, 3))
+
+
+def small_sums(lefts, rights, width):
+    terms = [over_tokens(left, right).astype(BF16) for left, right in zip(lefts, rights)]
+    used = sum(term.shape[1] for term in terms)
+    if width > used:
+        terms.append(jnp.zeros((terms[0].shape[0], width - used), BF16))
+    return jnp.concatenate(terms, 1).reshape(-1, 2, width // 2)
+
+
+def masked_scores(query_low, key_low, allowed, scale):
+    raw = jnp.einsum("thd,sd->hts", query_low, key_low, preferred_element_type=jnp.float32)
+    return jnp.where(allowed, raw * scale, -1e30)
+
+
+def attend(query, key, value, cosine, sine, query_g, key_g, allowed, scale):
+    count, dim = key.shape
+    heads = query.reshape(count, -1, dim)
+    query_low = rotate(rms_norm(heads, query_g), cosine, sine).astype(BF16)
+    key_low = rotate(rms_norm(key[:, None], key_g), cosine, sine).astype(BF16)[:, 0]
+    scores = masked_scores(query_low, key_low, allowed, scale)
+    most = jnp.max(scores, -1, keepdims=True)
+    log_total = most + jnp.log(jnp.sum(jnp.exp(scores - most), -1, keepdims=True))
+    probs = jnp.exp(scores - log_total).astype(BF16)
+    out = jnp.einsum("hts,sd->thd", probs, value, preferred_element_type=jnp.float32)
+    return out.reshape(count, -1), query_low, key_low, log_total
+
+
+def attend_back(
+    d_out, query, key, query_low, key_low, value, lse, cosine, sine, query_g, key_g, allowed, scale
+):
+    count, dim = key.shape
+    d_heads = d_out.astype(BF16).reshape(count, -1, dim)
+    probs = jnp.exp(masked_scores(query_low, key_low, allowed, scale) - lse)
+    d_probs = jnp.einsum("thd,sd->hts", d_heads, value, preferred_element_type=jnp.float32)
+    inner = jnp.sum(probs * d_probs, -1, keepdims=True)
+    d_scores = (probs * (d_probs - inner)).astype(BF16)
+    d_query = jnp.einsum("hts,sd->thd", d_scores, key_low, preferred_element_type=jnp.float32)
+    d_key = jnp.einsum("hts,thd->sd", d_scores, query_low, preferred_element_type=jnp.float32)
+    d_value = jnp.einsum(
+        "hts,thd->sd", probs.astype(BF16), d_heads, preferred_element_type=jnp.float32
+    )
+    d_query, d_query_g = norm_back(
+        query.reshape(count, -1, dim), query_g, rotate_back(d_query * scale, cosine, sine)
+    )
+    d_key, d_key_g = norm_back(
+        key[:, None], key_g, rotate_back((d_key * scale)[:, None], cosine, sine)
+    )
+    return d_query.reshape(count, -1), d_key[:, 0], d_value, d_query_g[None], d_key_g[None]
+
+
+def paired_plan(
+    tokens,
+    layer_inputs,
+    cotangent,
+    doc_lengths,
+    w_query,
+    w_key,
+    w_value,
+    w_output,
+    laurel_left,
+    laurel_right,
+    w_gate,
+    w_up,
+    w_down,
+    w_plgate,
+    w_plproj,
+    g_input,
+    g_query,
+    g_key,
+    g_attn,
+    g_laurel,
+    g_preffw,
+    g_ffw,
+    g_perlayer,
+):
+    f32 = jnp.float32
+    batch_at = lax.axis_index("batch")
+    y_at, x_at = batch_at // 2, batch_at % 2
+    core = lax.axis_index("seq")
+    depth = lax.axis_size("fsdp")
+    shards = lax.axis_size("batch") * lax.axis_size("seq") * depth
+    shard_at = (batch_at * 2 + core) * depth + lax.axis_index("fsdp")
+    rows = w_query.shape[0]
+    model = rows * shards
+    half_model, quarter_model = model // 2, model // 4
+    tok_rows = tokens.shape[1]
+    seq_rows = 2 * tok_rows
+    head_dim = g_query.shape[0] * shards
+    head_part = g_query.shape[0]
+    score_scale = head_dim ** (-0.5)
+    rank, pl_width = laurel_left.shape[1], w_plgate.shape[1]
+    ff_width = w_gate.shape[1]
+    ff_part = ff_width // 4
+    query_width, kv_width = w_query.shape[1] // 2, w_key.shape[1] // 2
+    small_used = 2 * rank + 2 * pl_width
+    small_width = -(-small_used // 256) * 256
+
+    own_gains = jnp.stack([g_input, g_attn, g_laurel, g_preffw, g_ffw, g_perlayer]).astype(f32)
+    head_gains = jnp.stack([g_query, g_key]).astype(f32)
+    table = jnp.zeros((8, model), f32)
+    table = lax.dynamic_update_slice(table, own_gains, (0, shard_at * rows))
+    table = lax.dynamic_update_slice(table, head_gains, (6, shard_at * head_part))
+    gain_table = sum_all(table)
+    query_g, key_g = gain_table[6:7, :head_dim], gain_table[7:8, :head_dim]
+    model_g = halves_by(y_at, gain_table[:6], 1)
+    input_g, attn_g, laurel_g, preffw_g, ffw_g, perlayer_g = [model_g[i] for i in range(6)]
+
+    def core_half(array):
+        pair = array.reshape(rows, 2, -1)
+        return pick(pair, 1, core), pick(pair, 1, 1 - core)
+
+    def ff_block(array):
+        parts = array.reshape(rows, 2, 2, ff_part)
+        keep, send = pick(parts, 2, core), pick(parts, 2, 1 - core)
+        both = in_order(core, keep, swap_core(send), 0)
+        return pick(both, 2, x_at), pick(both, 2, 1 - x_at)
+
+    def ff_exchange(keep, send):
+        return in_order(x_at, keep, swap_x(send), 0).reshape(4, rows, ff_part)
+
+    small_own = jnp.concatenate(
+        [
+            laurel_left,
+            laurel_right,
+            w_plgate,
+            w_plproj,
+            jnp.zeros((rows, small_width - small_used), BF16),
+        ],
+        1,
+    )
+    first_keep, first_send = zip(
+        *[core_half(entry) for entry in (w_query, w_key, w_value, small_own)]
+    )
+    first_keep = jnp.concatenate(first_keep, 1)
+    first_block = in_order(core, first_keep, swap_core(jnp.concatenate(first_send, 1)), 0)
+    first_z = jnp.concatenate(gather_z(first_block), 0)
+    out_keep, out_send = core_half(w_output)
+    gate_four = ff_exchange(*ff_block(w_gate))
+    up_keep, up_send = ff_block(w_up)
+    up_four = ff_exchange(up_keep, after(up_send, gate_four))
+    down_keep, down_send = ff_block(w_down)
+    down_four = ff_exchange(down_keep, after(down_send, up_four))
+    out_block = in_order(core, out_keep, swap_core(out_send), 0)
+    gate_z = gather_z(after(gate_four, first_block))
+    out_z = jnp.concatenate(gather_z(after(out_block, gate_four)), 0)
+    up_z = gather_z(after(up_four, out_block))
+    ff_half = ff_part // 2
+    down_later = after(down_four[:, :, ff_half:], up_four)
+    down_z = gather_z(down_later)
+    down_early = down_four[:, :, :ff_half]
+    down_both = jnp.concatenate([down_early, swap_y(down_early)], 0)
+    down_eight = gather_z(after(down_both, down_later))
+
+    resid_in = halves_by(y_at, tokens[0], 1).astype(f32)
+    upstream = halves_by(y_at, cotangent[0], 1).astype(f32)
+    perlayer = layer_inputs[0].astype(f32)
+    own_places = core * tok_rows + jnp.arange(tok_rows, dtype=jnp.int32)
+    other_places = (1 - core) * tok_rows + jnp.arange(tok_rows, dtype=jnp.int32)
+    places = jnp.concatenate([own_places, other_places])
+    segment, rel_pos = positions_of(places, doc_lengths[0])
+    cosine, sine = rope_tables(rel_pos, head_dim)
+    distance = places[:, None] - places[None, :]
+    allowed = (
+        (segment[:, None] == segment[None, :]) & (distance >= 0) & (distance < WINDOW)
+    )
+
+    def with_partner(own):
+        return jnp.concatenate([own, swap_core(own)], 0)
+
+    x_normed = rms_norm(resid_in, input_g)
+    x_low = x_normed.astype(BF16)
+    x_own_pairs = lax.optimization_barrier(to_pairs(x_at, x_low, 1))
+    first_z = after(first_z, (down_both, gain_table))
+    first_x, first_y = swap_x(first_z), swap_y(first_z)
+    x_pairs, cosine, sine, upstream = lax.optimization_barrier(
+        (with_partner(x_own_pairs), cosine, sine, upstream)
+    )
+    part = first_z.shape[0] // 2
+    first_corner = [
+        swap_y(after(first_x[:part], (x_pairs, cosine))),
+        swap_x(after(first_y[part:], (x_pairs, cosine))),
+    ]
+    first_w = jnp.concatenate([first_z, first_y, first_x] + first_corner, 0)
+    gate_far = chained(swap_y, gate_z, first_corner)
+
+    query_raw = project(x_pairs, first_w[:, :query_width])
+    key_raw = project(x_pairs, first_w[:, query_width : query_width + kv_width])
+    value_low = project(
+        x_pairs, first_w[:, query_width + kv_width : query_width + 2 * kv_width]
+    ).astype(BF16)
+    small_mine = first_w[:, query_width + 2 * kv_width :]
+    small_mine = after(small_mine, query_raw)
+    small_pair = in_order(core, small_mine, swap_core(small_mine), 0)
+    small_all = from_pairs(x_at, jnp.concatenate([small_pair[0], small_pair[1]], 1), 0)
+    left_w, right_w, plgate_w, plproj_w = split_columns(
+        small_all, [rank, rank, pl_width, pl_width]
+    )
+    out_z = after(out_z, query_raw)
+    query_raw = after(query_raw, gate_far[0])
+    out_x, out_y = swap_x(out_z), swap_y(out_z)
+    attn_heads, query_low, key_low, lse = attend(
+        query_raw, key_raw, value_low, cosine, sine, query_g[0], key_g[0], allowed, score_scale
+    )
+    out_x, out_y, attn_heads = lax.optimization_barrier(
+        (out_x, out_y, after(attn_heads, gate_far[1]))
+    )
+    attn_low = attn_heads.astype(BF16)
+    out_corner = [swap_y(out_x[:part]), swap_x(out_y[part:])]
+    output_w = jnp.concatenate([out_z, out_y, out_x] + out_corner, 0)
+    up_far = chained(swap_y, up_z, gate_far)
+    down_far = chained(swap_y, down_z, up_far)
+    def side_by_side(early, late):
+        whole = jnp.zeros((model, ff_part), BF16)
+        whole = lax.dynamic_update_slice(whole, jnp.concatenate(early, 0), (0, 0))
+        return lax.dynamic_update_slice(whole, jnp.concatenate(late, 0), (0, ff_half))
+
+    left_low = project(x_low, left_w).astype(BF16)
+    right_out = against_rows(left_low, right_w)
+    attn_keep, attn_send = onto_model([attn_low], [output_w])
+    attn_proj = from_pairs(x_at, attn_keep + swap_core(attn_send).astype(f32), 1)
+    hidden = (
+        resid_in + rms_norm(attn_proj, attn_g) + x_normed + rms_norm(right_out, laurel_g)
+    ) * ROOT_HALF
+
+    def sum_near_and_far(near_of, far):
+        far_sum = (far[0] + swap_core(far[1]).astype(f32)).astype(BF16)
+        crossed = swap_x(far_sum)
+        near = near_of(far_sum)
+        return near[0] + swap_core(near[1]).astype(f32), crossed, near
+
+    ffw_in = rms_norm(hidden, preffw_g).astype(BF16)
+    ffw_far = swap_x(ffw_in)
+    ffw_near = with_partner(ffw_in)
+    gate_w, up_w = [
+        jnp.concatenate([after(mine[0], ffw_near)] + mine[1:] + far, 0)
+        for mine, far in ((gate_z, gate_far), (up_z, up_far))
+    ]
+    gates_near, ups_near, act_near = gate_up_act(ffw_near, gate_w, up_w)
+    ffw_far = with_partner(after(ffw_far, act_near))
+    down_w = side_by_side([after(down_eight[0], act_near)] + down_eight[1:], down_z + down_far)
+    gates_far, ups_far, act_far = gate_up_act(after(ffw_far, down_far[0]), gate_w, up_w)
+    downs_far = onto_model([act_far], [down_w])
+    down_terms, crossed, _ = sum_near_and_far(
+        lambda earlier: onto_model([after(act_near, earlier)], [down_w]), downs_far
+    )
+    down_terms = down_terms + crossed.astype(f32)
+    second = hidden + rms_norm(down_terms, ffw_g)
+    second_low = second.astype(BF16)
+    plgate_out = project(second_low, plgate_w)
+    gated_low = geglu(plgate_out, perlayer).astype(BF16)
+    plproj_out = against_rows(gated_low, plproj_w)
+    mixed_out = halves_by(y_at, (second + rms_norm(plproj_out, perlayer_g)).astype(BF16), 1)
+
+    d_plproj, d_perlayer_g = norm_back(plproj_out, perlayer_g, upstream)
+    d_plproj_low = d_plproj.astype(BF16)
+    d_gated = project(d_plproj_low, plproj_w)
+    d_plgate_low = jax.vjp(geglu, plgate_out, perlayer)[1](d_gated)[0].astype(BF16)
+    d_second = upstream + against_rows(d_plgate_low, plgate_w)
+    d_down, d_ffw_g = norm_back(down_terms, ffw_g, d_second)
+    d_down_low = d_down.astype(BF16)
+    d_down_far = swap_x(d_down_low)
+    d_down_near = with_partner(d_down_low)
+    d_gate_near, d_up_near = gate_up_back(d_down_near, down_w, gates_near, ups_near)
+    d_down_far = with_partner(after(d_down_far, d_gate_near))
+
+    ff_split = (4, depth, rows)
+
+    def ff_send(sides, first_column=0, width=ff_part):
+        cut = [(left, [(right, first_column, width)]) for left, right in sides]
+        return weight_sum(cut, half_model, half_model, ff_split)
+
+    def ff_keep(sides, received, first_column=0, width=ff_part):
+        cut = [(left, [(right, first_column, width)]) for left, right in sides]
+        return weight_sum(cut, 0, half_model, ff_split, received, True)
+
+    def ff_owned(four):
+        four = four.reshape(2, 2, rows, ff_part)
+        keep, send = pick(four, 0, x_at), pick(four, 0, 1 - x_at)
+        over = swap_x(send)
+        a, b = pick(keep, 0, core), pick(over, 0, core)
+        crossed = swap_core(jnp.stack([pick(keep, 0, 1 - core), pick(over, 0, 1 - core)]))
+        quarters = []
+        for x_of in range(2):
+            near = jnp.where(x_at == x_of, a, b)
+            far = jnp.where(x_at == x_of, crossed[0], crossed[1])
+            quarters += [
+                jnp.where(core == c_of, near, far).astype(f32) for c_of in range(2)
+            ]
+        return jnp.concatenate(quarters, 1)
+
+    down_sides = [(d_down_near, act_near), (d_down_far, act_far)]
+    down_sent = ff_send(down_sides, ff_half, ff_half)
+    down_near = chained(swap_y, down_sent)
+    whole_cut = [(left, [(right, 0, ff_half)]) for left, right in down_sides]
+    down_whole = weight_sum(whole_cut, 0, model, (8, depth, rows), (), True)
+    down_eight = scatter_z(down_whole)
+    d_gate_far, d_up_far = gate_up_back(
+        d_down_far, down_w, after(gates_far, down_near[0]), ups_far
+    )
+    gate_sides = [(ffw_near, d_gate_near), (ffw_far, d_gate_far)]
+    up_sides = [(ffw_near, d_up_near), (ffw_far, d_up_far)]
+    ffw_weights = [gate_w, up_w]
+    gate_sent = ff_send(gate_sides)
+    gate_near = chained(swap_y, gate_sent, down_near)
+    d_ffw_far = onto_model([d_gate_far, d_up_far], ffw_weights)
+    d_ffw_terms, crossed, d_ffw_near = sum_near_and_far(
+        lambda earlier: onto_model(
+            [after(d_gate_near, (earlier, gate_near[0], down_eight)), d_up_near], ffw_weights
+        ),
+        d_ffw_far,
+    )
+    up_sent = ff_send(up_sides)
+    up_near = chained(swap_y, up_sent, gate_near)
+    down_near = [after(down_near[0], up_sent)] + down_near[1:]
+    down_kept = ff_keep(down_sides, down_near, ff_half, ff_half)
+    down_four = scatter_z(down_kept)
+    gate_near = [after(gate_near[0], down_kept)] + gate_near[1:]
+    gate_kept = ff_keep(gate_sides, gate_near)
+    gate_four = scatter_z(gate_kept)
+    d_ffw_terms = d_ffw_terms + after(crossed, gate_kept).astype(f32)
+
+    d_hidden_norm, d_preffw_g = norm_back(hidden, preffw_g, d_ffw_terms)
+    d_branch = (d_second + d_hidden_norm) * ROOT_HALF
+    d_laurel, d_laurel_g = norm_back(right_out, laurel_g, d_branch)
+    d_laurel_low = d_laurel.astype(BF16)
+    d_left_low = project(d_laurel_low, right_w).astype(BF16)
+    d_attn, d_attn_g = norm_back(attn_proj, attn_g, d_branch)
+    d_attn_pairs = with_partner(lax.optimization_barrier(to_pairs(x_at, d_attn.astype(BF16), 1)))
+
+    pair_split = (2, depth, rows)
+
+    def whole_columns(keep, received):
+        ends = [jnp.where(core == c_of, keep, received).astype(f32) for c_of in range(2)]
+        return jnp.concatenate(ends, 1)
+
+    def pair_owned(pair):
+        pair = pair.reshape(2, rows, pair.shape[1])
+        keep, send = pick(pair, 0, core), pick(pair, 0, 1 - core)
+        return keep, swap_core(send)
+
+    def pair_send(sides):
+        return weight_sum(sides, half_model, half_model, pair_split)
+
+    def pair_pass(sides, over_x):
+        return weight_sum(sides, quarter_model, quarter_model, pair_split, over_x[2:])
+
+    def pair_keep(sides, over_x, over_y):
+        got = list(zip(over_x[:2], over_y))
+        return weight_sum(sides, 0, quarter_model, pair_split, got, True)
+
+    out_sides = [(d_attn_pairs, [(attn_low, 0, query_width)])]
+    out_sent = pair_send(out_sides)
+    out_near = chained(swap_x, out_sent[2:] + out_sent[:2])
+    out_near = out_near[2:] + out_near[:2]
+    d_heads = project(d_attn_pairs, output_w)
+    d_heads = after(d_heads, (up_near[1], down_four))
+    d_query_low, d_key_low, d_value_low, d_query_g, d_key_g = attend_back(
+        d_heads,
+        query_raw,
+        key_raw,
+        query_low,
+        key_low,
+        value_low,
+        lse,
+        cosine,
+        sine,
+        query_g[0],
+        key_g[0],
+        allowed,
+        score_scale,
+    )
+
+    d_query_low, d_key_low, d_value_low = [
+        entry.astype(BF16) for entry in (d_query_low, d_key_low, d_value_low)
+    ]
+    first_rights = [
+        (d_query_low, 0, query_width),
+        (d_key_low, 0, kv_width),
+        (d_value_low, 0, kv_width),
+    ]
+    first_sides = [(x_pairs, first_rights)]
+    first_sent = pair_send(first_sides)
+    first_near = chained(swap_x, first_sent[2:] + first_sent[:2], out_near[:2])
+    first_near = first_near[2:] + first_near[:2]
+    up_kept = ff_keep(up_sides, up_near)
+    up_four = scatter_z(up_kept)
+    small_halves = small_sums(
+        [x_low, d_laurel_low, second_low, d_plproj_low],
+        [d_left_low, left_low, d_plgate_low, gated_low],
+        small_width,
+    )
+    small_sum = pick(small_halves, 1, core).astype(f32) + swap_core(
+        pick(small_halves, 1, 1 - core)
+    ).astype(f32)
+    small_sum = small_sum.astype(BF16).reshape(2, 2, quarter_model, small_width // 2)
+    over_x = swap_x(pick(small_sum, 1, 1 - x_at))
+    small_sum = pick(small_sum, 1, x_at).astype(f32) + over_x.astype(f32)
+    small_sum = small_sum[0] + swap_y(small_sum[1].astype(BF16)).astype(f32)
+    small_sum = small_sum.reshape(2, depth, rows, small_width // 2).astype(BF16)
+    small_pair = scatter_z_small(jnp.transpose(small_sum, (1, 0, 2, 3)))
+    small_keep, small_send = pick(small_pair, 0, core), pick(small_pair, 0, 1 - core)
+    out_right = out_sides[0][1]
+    out_near = out_near[:2] + [after(out_near[2], up_kept), out_near[3]]
+    out_passed = pair_pass([(d_attn_pairs, out_right)], out_near)
+    out_over = chained(swap_y, out_passed, up_near)
+    first_w_parts = split_columns(
+        first_w[:, : query_width + 2 * kv_width], [query_width, kv_width, kv_width]
+    )
+    d_x_keep, d_x_send = onto_model([d_query_low, d_key_low, d_value_low], first_w_parts)
+    d_x_terms = from_pairs(x_at, d_x_keep + swap_core(d_x_send).astype(f32), 1)
+    d_x_terms = d_x_terms + against_rows(d_left_low, left_w)
+    d_input, d_input_g = norm_back(resid_in, input_g, d_x_terms + d_branch)
+    grad_tokens = halves_by(y_at, d_input + d_branch, 1)[None]
+
+    widths = [query_width, kv_width, kv_width]
+    first_passed = pair_pass([(x_pairs, first_rights)], first_near)
+    first_over = chained(swap_y, first_passed, out_over)
+    out_over = [after(out_over[0], up_four)] + out_over[1:]
+    out_kept = pair_keep([(d_attn_pairs, out_right)], out_near, out_over)
+    out_four = scatter_z(out_kept)
+    first_kept = pair_keep([(x_pairs, first_rights)], first_near, first_over)
+    first_four = scatter_z(first_kept)
+    grad_output = whole_columns(*pair_owned(out_four))
+    first_keep, first_received = pair_owned(first_four)
+    grad_query, grad_key, grad_value = [
+        whole_columns(keep, received)
+        for keep, received in zip(
+            split_columns(first_keep, widths), split_columns(first_received, widths)
+        )
+    ]
+
+    grad_left, grad_right, grad_plgate, grad_plproj = split_columns(
+        whole_columns(small_keep, swap_core(small_send)), [rank, rank, pl_width, pl_width]
+    )
+
+    down_eight, down_four = after((down_eight, down_four), d_query_low)
+    down_eight = down_eight.reshape(2, 4, rows, ff_half)
+    down_last = down_eight[0].astype(f32) + swap_y(down_eight[1]).astype(f32)
+    grad_down = ff_owned(
+        jnp.concatenate([down_last.astype(BF16), down_four.reshape(4, rows, ff_half)], 2)
+    )
+    grad_gate = ff_owned(after(gate_four, out_passed))
+    grad_up = ff_owned(up_four)
+
+    gain_grads = jnp.stack(
+        [d_input_g, d_attn_g, d_laurel_g, d_preffw_g, d_ffw_g, d_perlayer_g]
+    )
+    head_grads = jnp.pad(
+        jnp.concatenate([d_query_g, d_key_g], 0), ((0, 0), (0, model - head_dim))
+    )
+    gain_sums = sum_all(jnp.concatenate([halves_by(y_at, gain_grads, 1), head_grads], 0))
+    own_sums = lax.dynamic_slice(gain_sums, (0, shard_at * rows), (6, rows))
+    own_heads = lax.dynamic_slice(gain_sums, (6, shard_at * head_part), (2, head_part))
+    (
+        grad_g_input,
+        grad_g_attn,
+        grad_g_laurel,
+        grad_g_preffw,
+        grad_g_ffw,
+        grad_g_perlayer,
+    ) = [own_sums[i] for i in range(6)]
+    grad_g_query, grad_g_key = own_heads[0], own_heads[1]
+    return (
+        mixed_out[None],
+        grad_tokens,
+        grad_query,
+        grad_key,
+        grad_value,
+        grad_output,
+        grad_left,
+        grad_right,
+        grad_gate,
+        grad_up,
+        grad_down,
+        grad_plgate,
+        grad_plproj,
+        grad_g_input,
+        grad_g_query,
+        grad_g_key,
+        grad_g_attn,
+        grad_g_laurel,
+        grad_g_preffw,
+        grad_g_ffw,
+        grad_g_perlayer,
+    )
+
+
 def solution(mesh):
-    placed = (
-        P(("batch", "fsdp"), "seq", None),
-        P(("batch", "fsdp"), "seq", None),
-        P(("batch", "fsdp"), "seq", None),
-        P(("batch", "fsdp"), None),
-        P(("batch", "seq", "fsdp"), None),
-        P(("batch", "seq", "fsdp"), None),
-        P(("batch", "seq", "fsdp"), None),
-        P(("batch", "seq", "fsdp"), None),
-        P(("batch", "seq", "fsdp"), None),
-        P(("batch", "seq", "fsdp"), None),
-        P(("batch", "seq", "fsdp"), None),
-        P(("batch", "seq", "fsdp"), None),
-        P(("batch", "seq", "fsdp"), None),
-        P(("batch", "seq", "fsdp"), None),
-        P(("batch", "seq", "fsdp"), None),
-        P(("batch", "seq", "fsdp")),
-        P(("batch", "seq", "fsdp")),
-        P(("batch", "seq", "fsdp")),
-        P(("batch", "seq", "fsdp")),
-        P(("batch", "seq", "fsdp")),
-        P(("batch", "seq", "fsdp")),
-        P(("batch", "seq", "fsdp")),
-        P(("batch", "seq", "fsdp")),
-    )
+    paired = mesh.shape["batch"] == 4 and mesh.shape["seq"] == 2
+    by_token = P(ROW_AXES, "seq", None)
+    by_row = P(ALL_AXES, None)
+    by_entry = P(ALL_AXES)
     return jax.shard_map(
-        local,
+        paired_plan if paired else whole_gather_plan,
         mesh=mesh,
-        in_specs=placed,
-        out_specs=(
-            P(("batch", "fsdp"), "seq", None),
-            P(("batch", "fsdp"), "seq", None),
-            P(("batch", "seq", "fsdp"), None),
-            P(("batch", "seq", "fsdp"), None),
-            P(("batch", "seq", "fsdp"), None),
-            P(("batch", "seq", "fsdp"), None),
-            P(("batch", "seq", "fsdp"), None),
-            P(("batch", "seq", "fsdp"), None),
-            P(("batch", "seq", "fsdp"), None),
-            P(("batch", "seq", "fsdp"), None),
-            P(("batch", "seq", "fsdp"), None),
-            P(("batch", "seq", "fsdp"), None),
-            P(("batch", "seq", "fsdp"), None),
-            P(("batch", "seq", "fsdp")),
-            P(("batch", "seq", "fsdp")),
-            P(("batch", "seq", "fsdp")),
-            P(("batch", "seq", "fsdp")),
-            P(("batch", "seq", "fsdp")),
-            P(("batch", "seq", "fsdp")),
-            P(("batch", "seq", "fsdp")),
-            P(("batch", "seq", "fsdp")),
-        ),
+        in_specs=(by_token,) * 3 + (P(ROW_AXES, None),) + (by_row,) * 11 + (by_entry,) * 8,
+        out_specs=(by_token,) * 2 + (by_row,) * 11 + (by_entry,) * 8,
         check_vma=False,
     )

time: 3290 us -> 1420 us (0.43)
  waiting for transfers between devices: 2290 us -> 520 us
  blocking collectives: 231 us -> 0 us
  starting transfers between devices: 3.68 us -> 94.5 us
  local copies, waits for them, and re-layouts: 113 us -> 202 us
  other arithmetic: 206 us -> 151 us
    reduce_scatter x1 -> x6, waiting for transfers between devices: 1600 us -> 13.3 us  [scatter_z(): return lax.psum_scatter(flat, 'fsdp', scatter_dimension=0, tiled=True)]
    all_gather x9 -> x6, waiting for transfers between devices: 592 us -> 14.5 us  [gather_z(): stacked = lax.all_gather(array, 'fsdp', axis=0, tiled=False)]
    ppermute x2 -> x98, waiting for transfers between devices: 0.01 us -> 491 us  [the longest x37 269 us: swap_y(): return lax.ppermute(array, 'batch', Y_PAIRS)]
    all_gather x2 -> x0, blocking collectives: 143 us -> none  [the longest x1 71.9 us: local(): lax.all_gather(laurel_right, ('batch', 'seq', 'fsdp'), axis=0, tiled=True)]
    concatenate x3 -> x22, other arithmetic: 134 us -> 20.5 us  [the longest x1 4.8 us: with_partner(): return jnp.concatenate([own, swap_core(own)], 0)]
    unnamed x12, waiting for transfers between devices: 95.4 us -> 0.86 us
    ppermute x2 -> x98, starting transfers between devices: 3.26 us -> 93.4 us  [the longest x37 44.2 us: swap_y(): return lax.ppermute(array, 'batch', Y_PAIRS)]
    unnamed x2 -> x0, blocking collectives: 87.8 us -> none
  transfers between devices with their start and end apart: 13 -> 110, of which waited for: 8 -> 52; matrix products, arithmetic and copies ran while one was open for 15% -> 45% of each run, Pallas kernels for 0% -> 0%
where the time goes in v1:
time: 1420 us
  waiting for transfers between devices  520 us (37%)
  matrix products  430 us (30%)
  local copies, waits for them, and re-layouts  202 us (14%)
  other arithmetic  151 us (11%)
  starting transfers between devices  94.5 us (7%)
  between operations  18 us (1%)
    ppermute x37, waiting for transfers between devices, swap_y(): return lax.ppermute(array, 'batch', Y_PAIRS)  269 us
    ppermute x25, waiting for transfers between devices, swap_x(): return lax.ppermute(array, 'batch', X_PAIRS)  198 us
    dot_general x24, matrix products, against_rows(): lax.dot_general(left, right, (((1,), (1,)), ((), ())), preferred_element_...  148 us
    dot_general x30, matrix products, over_tokens(): lax.dot_general(left, right, (((0,), (0,)), ((), ())), preferred_element_...  121 us
    dot_general x14, matrix products, project(): return jnp.dot(left, right, preferred_element_type=jnp.float32)  112 us
    unnamed x504, local copies, waits for them, and re-layouts  93.4 us
    ppermute x37, starting transfers between devices, swap_y(): return lax.ppermute(array, 'batch', Y_PAIRS)  44.2 us
    ppermute x25, starting transfers between devices, swap_x(): return lax.ppermute(array, 'batch', X_PAIRS)  31.6 us
  transfers between devices with their start and end apart: 110, of which 52 were waited for; matrix products, arithmetic and copies ran while one was open for 45% of the time, Pallas kernels for 0%

profile of v1, /device:TPU:0, one launch (start us, length us, event | category | flops | bytes accessed | tf_op | source)
XLA Modules:
  0.0 1416.4 jit_solution(1143730698414940456)
XLA Ops:
  28.7 10.3 collective-permute-done.2
  62.2 13.8 collective-permute-done.4
  98.2 9.9 collective-permute-done.14
  112.5 8.5 collective-permute-done.15
  145.3 22.1 %collective-permute-done.17 = bf16[512,1920]{1,0:T(8,128)(2,1)} collective-permute-done((bf16[512,1920]{1,0:T(8,128)(2,1)}, bf16[512,1920]{1,0:T(8,128)(2,1)}, u32[]{:S(2)}, u32[]{:S(2)}) %collective-permute-start.17) | collective-permute-done | bytes 1966112 | tf_op jit(solution)/shard_map/ppermute | solution.py:410
  181.7 8.1 collective-permute-done.18
  222.2 32.1 %collective-permute-done.22 = bf16[256,2048]{1,0:T(8,128)(2,1)} collective-permute-done((bf16[256,2048]{1,0:T(8,128)(2,1)S(1)}, bf16[256,2048]{1,0:T(8,128)(2,1)}, u32[]{:S(2)}, u32[]{:S(2)}) %collective-permute-start.22) | collective-permute-done | bytes 1048608 | tf_op jit(solution)/shard_map/ppermute | solution.py:414
  270.2 7.9 fusion.345
  278.2 8.1 exponential_reduce_fusion
  286.3 8.6 fusion.80
  322.2 18.6 %collective-permute-done.29 = bf16[256,2048]{1,0:T(8,128)(2,1)} collective-permute-done((bf16[256,2048]{1,0:T(8,128)(2,1)}, bf16[256,2048]{1,0:T(8,128)(2,1)}, u32[]{:S(2)}, u32[]{:S(2)}) %collective-permute-start.29) | collective-permute-done | bytes 1048608 | tf_op jit(solution)/shard_map/ppermute | solution.py:414
  342.1 21.1 %collective-permute-done.30 = bf16[256,2048]{1,0:T(8,128)(2,1)} collective-permute-done((bf16[256,2048]{1,0:T(8,128)(2,1)}, bf16[256,2048]{1,0:T(8,128)(2,1)}, u32[]{:S(2)}, u32[]{:S(2)}) %collective-permute-start.30) | collective-permute-done | bytes 1048608 | tf_op jit(solution)/shard_map/ppermute | solution.py:414
  387.0 21.1 %collective-permute-done.32 = bf16[256,2048]{1,0:T(8,128)(2,1)S(1)} collective-permute-done((bf16[256,2048]{1,0:T(8,128)(2,1)S(1)}, bf16[256,2048]{1,0:T(8,128)(2,1)S(1)}, u32[]{:S(2)}, u32[]{:S(2)}) %collective-permute-start.32) | collective-permute-done | bytes 1048608 | tf_op jit(solution)/shard_map/ppermute | solution.py:414
  413.3 17.3 %collective-permute-done.33 = bf16[256,2048]{1,0:T(8,128)(2,1)} collective-permute-done((bf16[256,2048]{1,0:T(8,128)(2,1)S(1)}, bf16[256,2048]{1,0:T(8,128)(2,1)}, u32[]{:S(2)}, u32[]{:S(2)}) %collective-permute-start.33) | collective-permute-done | bytes 1048608 | tf_op jit(solution)/shard_map/ppermute | solution.py:414
  432.0 21.1 %collective-permute-done.34 = bf16[256,2048]{1,0:T(8,128)(2,1)} collective-permute-done((bf16[256,2048]{1,0:T(8,128)(2,1)S(1)}, bf16[256,2048]{1,0:T(8,128)(2,1)}, u32[]{:S(2)}, u32[]{:S(2)}) %collective-permute-start.34) | collective-permute-done | bytes 1048608 | tf_op jit(solution)/shard_map/ppermute | solution.py:414
  465.7 9.8 collective-permute-done.38
  494.5 13.2 fusion.322
  507.7 16.6 %fusion.20 = (bf16[1024,2048]{1,0:T(8,128)(2,1)}, bf16[1024,2048]{1,0:T(8,128)(2,1)}) fusion(f32[1024,2048]{1,0:T(8,128)} %fusion.322, bf16[2048,2048]{1,0:T(8,128)(2,1)S(1)} %constant_dynamic-update-slice_fusion.18, bf16[512,2048]{1,0:T(8,128)(2,1)} %collective-permute-done.28, bf16[512,2048]{1,0:T(8,128)(2,1)} %multiply_convert_fusion), kind=kOutput, calls=%fused_computation.37 | convolution fusion | flops 8621391872 | bytes 29360128 | tf_op jit(solution)/shard_map/dot_general | solution.py:78
  524.4 14.4 %all-gather.23.cloned.1.call-done = bf16[32,64,1024]{2,1,0:T(8,128)(2,1)} async-done(((bf16[8,64,1024]{2,1,0:T(8,128)(2,1)}), bf16[32,64,1024]{2,1,0:T(8,128)(2,1)}) %all-gather.23.cloned.1.call-update) | async-done | bytes 4194320 | tf_op jit(solution)/shard_map/all_gather | solution.py:479
  558.9 8.9 fusion.346
  567.8 13.1 fusion.327
  580.9 8.7 convolution_convert_fusion.2
  593.9 8.1 add_convert_fusion.12
  602.0 8.7 convolution_convert_fusion.1
  612.4 7.4 fusion.120
  619.9 38.9 %collective-permute-done.43 = bf16[512,2048]{1,0:T(8,128)(2,1)S(1)} collective-permute-done((bf16[512,2048]{1,0:T(8,128)(2,1)S(1)}, bf16[512,2048]{1,0:T(8,128)(2,1)S(1)}, u32[]{:S(2)}, u32[]{:S(2)}) %collective-permute-start.43) | collective-permute-done | bytes 2097184 | tf_op jit(solution)/shard_map/ppermute | solution.py:410
  685.6 22.3 %fusion.36 = (bf16[1024,2048]{1,0:T(8,128)(2,1)}, bf16[1024,2048]{1,0:T(8,128)(2,1)}) fusion(f32[1024,2048]{1,0:T(8,128)} %fusion.322, bf16[1024,2048]{1,0:T(8,128)(2,1)} %get-tuple-element.388, bf16[2048,1024]{1,0:T(8,128)(2,1)} %constant_dynamic-update-slice_fusion.36, bf16[2048,1024]{1,0:T(8,128)(2,1)} %constant_dynamic-update-slice_fusion.28, ...), kind=kOutput, calls=%fused_computation.53 | convolution fusion | flops 8671723520 | bytes 33554432 | tf_op jit(solution)/shard_map/dot_general | solution.py:78
  707.8 22.9 %collective-permute-done.45 = bf16[512,2048]{1,0:T(8,128)(2,1)} collective-permute-done((bf16[512,2048]{1,0:T(8,128)(2,1)}, bf16[512,2048]{1,0:T(8,128)(2,1)}, u32[]{:S(2)}, u32[]{:S(2)}) %collective-permute-start.45) | collective-permute-done | bytes 2097184 | tf_op jit(solution)/shard_map/ppermute | solution.py:410
  732.6 9.5 fusion.100
  742.1 9.6 fusion.98
  752.0 15.1 %fusion.323 = f32[1024,2048]{1,0:T(8,128)} fusion(bf16[1024,2048]{1,0:T(8,128)(2,1)S(1)} %constant_dynamic-update-slice_fusion.44, bf16[2048,1024]{1,0:T(8,128)(2,1)} %constant_dynamic-update-slice_fusion.36, bf16[2048,1024]{1,0:T(8,128)(2,1)} %constant_dynamic-update-slice_fusion.28), kind=kOutput, calls=%fused_computation.692 | convolution fusion | flops 8606711808 | bytes 20971520 | tf_op jit(solution)/shard_map/dot_general | solution.py:78
  769.5 7.2 fusion.102
  784.0 8.3 add_convert_fusion.3
  801.7 10.4 fusion.8
  812.1 11.3 fusion.105
  823.4 7.0 fusion.131
  832.5 10.1 add_convert_fusion.9
  842.6 7.1 fusion.133
  849.6 7.2 fusion.127
  856.9 10.0 fusion.108
  866.8 10.0 fusion.110
  876.8 6.8 add_convert_fusion.2
  883.6 7.9 add_convert_fusion.4
  904.8 14.7 %collective-permute-done.55 = bf16[256,2048]{1,0:T(8,128)(2,1)} collective-permute-done((bf16[256,2048]{1,0:T(8,128)(2,1)}, bf16[256,2048]{1,0:T(8,128)(2,1)}, u32[]{:S(2)}, u32[]{:S(2)}) %collective-permute-start.55) | collective-permute-done | bytes 1048608 | tf_op jit(solution)/shard_map/ppermute | solution.py:414
  921.0 20.9 %collective-permute-done.50 = bf16[256,2048]{1,0:T(8,128)(2,1)} collective-permute-done((bf16[256,2048]{1,0:T(8,128)(2,1)S(1)}, bf16[256,2048]{1,0:T(8,128)(2,1)}, u32[]{:S(2)}, u32[]{:S(2)}) %collective-permute-start.50) | collective-permute-done | bytes 1048608 | tf_op jit(solution)/shard_map/ppermute | solution.py:414
  943.5 11.5 fusion.129
  966.0 20.9 %collective-permute-done.56 = bf16[256,2048]{1,0:T(8,128)(2,1)} collective-permute-done((bf16[256,2048]{1,0:T(8,128)(2,1)}, bf16[256,2048]{1,0:T(8,128)(2,1)}, u32[]{:S(2)}, u32[]{:S(2)}) %collective-permute-start.56) | collective-permute-done | bytes 1048608 | tf_op jit(solution)/shard_map/ppermute | solution.py:414
  988.4 11.2 add_convert_fusion.7
  999.6 9.0 add_convert_fusion.1
  1011.6 20.3 %collective-permute-done.69 = bf16[256,2048]{1,0:T(8,128)(2,1)} collective-permute-done((bf16[256,2048]{1,0:T(8,128)(2,1)}, bf16[256,2048]{1,0:T(8,128)(2,1)}, u32[]{:S(2)}, u32[]{:S(2)}) %collective-permute-start.69) | collective-permute-done | bytes 1048608 | tf_op jit(solution)/shard_map/ppermute | solution.py:414
  1033.4 10.6 fusion.117
  1044.2 7.1 multiply_reduce_fusion.3
  1076.5 8.5 add_convert_fusion
  1095.5 7.9 fusion.50
  1103.5 14.3 %fusion = (f32[4,1024]{1,0:T(4,128)S(1)}, f32[1024,1024,4]{1,0,2:T(8,128)}) fusion(f32[4,1024,1024]{1,2,0:T(8,128)} %get-tuple-element.386, f32[4,1024]{1,0:T(4,128)S(1)} %copy-done.109, bf16[1024,256,1]{1,0,2:T(8,128)(2,1)S(1)} %copy-done.113, bf16[128,4,8,256]{3,2,1,0:T(8,128)(2,1)} %bitcast.544), kind=kOutput, calls=%fused_computation.2 | convolution fusion | flops 2160062464 | bytes 36208640 | tf_op jit(solution)/shard_map/thd,sd->hts/dot_general | solution.py:590
  1120.6 10.6 fusion.2
  1137.1 9.0 multiply_bitcast_fusion
  1231.4 7.5 collective-permute-done.90
  1243.0 7.2 collective-permute-done.85
  1261.5 11.2 collective-permute-done.62
  1291.6 9.2 collective-permute-done.67
  1301.9 15.7 %collective-permute-done.63 = bf16[256,1536]{1,0:T(8,128)(2,1)S(1)} collective-permute-done((bf16[256,1536]{1,0:T(8,128)(2,1)}, bf16[256,1536]{1,0:T(8,128)(2,1)S(1)}, u32[]{:S(2)}, u32[]{:S(2)}) %collective-permute-start.63) | collective-permute-done | bytes 786464 | tf_op jit(solution)/shard_map/ppermute | solution.py:410
  1339.0 12.0 collective-permute-done.64
  1391.3 13.2 reduce-scatter.11.cloned.1.call-done
  (983 shorter events, 586.6 us)
Async XLA Ops:
  7.2 114.9 %all-gather.15.cloned.1.call-start = ((), (), s32[]{:S(2)}) async-start(), calls=%async_computation.13 | async-start | bytes 2457600 | tf_op jit(solution)/shard_map/all_gather | solution.py:479
  15.8 155.3 %all-gather.13.cloned.1.call-start = ((), (), s32[]{:S(2)}) async-start(), calls=%async_computation.12 | async-start | bytes 1310720 | tf_op jit(solution)/shard_map/all_gather | solution.py:479
  41.2 164.7 %all-gather.17.cloned.1.call-start = ((), (), s32[]{:S(2)}) async-start(), calls=%async_computation.14 | async-start | bytes 5242880 | tf_op jit(solution)/shard_map/all_gather | solution.py:479
  41.9 277.4 %all-gather.19.cloned.1.call-start = ((), (), s32[]{:S(2)}) async-start(), calls=%async_computation.15 | async-start | bytes 5242880 | tf_op jit(solution)/shard_map/all_gather | solution.py:479
  52.7 40.6 %collective-permute-start.11 = (bf16[64,2,2048]{2,0,1:T(8,128)(2,1)}, bf16[64,2,2048]{2,0,1:T(8,128)(2,1)}, u32[]{:S(2)}, u32[]{:S(2)}) collective-permute-start(bf16[64,2,2048]{2,0,1:T(8,128)(2,1)} %bitcast.509), channel_id=1, source_target_pairs={{0,4},{4,0},{1,5},{5,1},{2,6},{6,2},{3,7},{7,3},{8,12},{12,8},{9,1... | collective-permute-start | bytes 1572872 | tf_op jit(solution)/shard_map/ppermute | solution.py:418
  87.4 323.0 %all-gather.21.cloned.1.call-start = ((), (), s32[]{:S(2)}) async-start(), calls=%async_computation.16 | async-start | bytes 2621440 | tf_op jit(solution)/shard_map/all_gather | solution.py:479
  125.3 42.2 %collective-permute-start.17 = (bf16[512,1920]{1,0:T(8,128)(2,1)}, bf16[512,1920]{1,0:T(8,128)(2,1)}, u32[]{:S(2)}, u32[]{:S(2)}) collective-permute-start(bf16[512,1920]{1,0:T(8,128)(2,1)} %pad_maximum_fusion.15), channel_id=1, source_target_pairs={{0,8},{8,0},{16,24},{24,16},{1,9},{9,1},{17,25},{25,17},{2,10},{10... | collective-permute-start | bytes 5898248 | tf_op jit(solution)/shard_map/ppermute | solution.py:410
  126.8 46.6 %collective-permute-start.16 = (bf16[512,1920]{1,0:T(8,128)(2,1)}, bf16[512,1920]{1,0:T(8,128)(2,1)}, u32[]{:S(2)}, u32[]{:S(2)}) collective-permute-start(bf16[512,1920]{1,0:T(8,128)(2,1)} %pad_maximum_fusion.15), channel_id=1, source_target_pairs={{0,16},{16,0},{8,24},{24,8},{1,17},{17,1},{9,25},{25,9},{2,18},{18... | collective-permute-start | bytes 5898248 | tf_op jit(solution)/shard_map/ppermute | solution.py:414
  136.2 402.7 %all-gather.23.cloned.1.call-start = ((), (), s32[]{:S(2)}) async-start(), calls=%async_computation.17 | async-start | bytes 5242880 | tf_op jit(solution)/shard_map/all_gather | solution.py:479
  204.0 91.0 %collective-permute-start.20 = (bf16[512,1024]{1,0:T(8,128)(2,1)}, bf16[512,1024]{1,0:T(8,128)(2,1)}, u32[]{:S(2)}, u32[]{:S(2)}) collective-permute-start(bf16[512,1024]{1,0:T(8,128)(2,1)} %pad_maximum_fusion.25), channel_id=1, source_target_pairs={{0,8},{8,0},{16,24},{24,16},{1,9},{9,1},{17,25},{25,17},{2,10},{10... | collective-permute-start | bytes 3145736 | tf_op jit(solution)/shard_map/ppermute | solution.py:410
  205.4 89.6 %collective-permute-start.21 = (bf16[512,1024]{1,0:T(8,128)(2,1)}, bf16[512,1024]{1,0:T(8,128)(2,1)}, u32[]{:S(2)}, u32[]{:S(2)}) collective-permute-start(bf16[512,1024]{1,0:T(8,128)(2,1)} %pad_maximum_fusion.25), channel_id=1, source_target_pairs={{0,16},{16,0},{8,24},{24,8},{1,17},{17,1},{9,25},{25,9},{2,18},{18... | collective-permute-start | bytes 3145736 | tf_op jit(solution)/shard_map/ppermute | solution.py:414
  210.0 44.3 %collective-permute-start.22 = (bf16[256,2048]{1,0:T(8,128)(2,1)S(1)}, bf16[256,2048]{1,0:T(8,128)(2,1)}, u32[]{:S(2)}, u32[]{:S(2)}) collective-permute-start(bf16[256,2048]{1,0:T(8,128)(2,1)S(1)} %bitcast.559), channel_id=1, source_target_pairs={{0,16},{16,0},{8,24},{24,8},{1,17},{17,1},{9,25},{25,9},{2,18},{18... | collective-permute-start | bytes 3145736 | tf_op jit(solution)/shard_map/ppermute | solution.py:414
  216.7 82.4 %collective-permute-start.27 = (bf16[2048,384]{1,0:T(8,128)(2,1)}, bf16[2048,384]{1,0:T(8,128)(2,1)}, u32[]{:S(2)}, u32[]{:S(2)}) collective-permute-start(bf16[2048,384]{1,0:T(8,128)(2,1)} %slice.571), channel_id=1, source_target_pairs={{0,4},{4,0},{1,5},{5,1},{2,6},{6,2},{3,7},{7,3},{8,12},{12,8},{9,1... | collective-permute-start | bytes 4718600 | tf_op jit(solution)/shard_map/ppermute | solution.py:418
  221.2 73.7 %collective-permute-start.23 = (bf16[256,2048]{1,0:T(8,128)(2,1)}, bf16[256,2048]{1,0:T(8,128)(2,1)}, u32[]{:S(2)}, u32[]{:S(2)}) collective-permute-start(bf16[256,2048]{1,0:T(8,128)(2,1)} %bitcast.68), channel_id=1, source_target_pairs={{0,16},{16,0},{8,24},{24,8},{1,17},{17,1},{9,25},{25,9},{2,18},{18... | collective-permute-start | bytes 3145736 | tf_op jit(solution)/shard_map/ppermute | solution.py:414
  311.4 53.2 %collective-permute-start.26 = (bf16[512,2048]{1,0:T(8,128)(2,1)}, bf16[512,2048]{1,0:T(8,128)(2,1)}, u32[]{:S(2)}, u32[]{:S(2)}) collective-permute-start(bf16[512,2048]{1,0:T(8,128)(2,1)} %convolution_convert_fusion), channel_id=1, source_target_pairs={{0,4},{4,0},{1,5},{5,1},{2,6},{6,2},{3,7},{7,3},{8,12},{12,8},{9,1... | collective-permute-start | bytes 6291464 | tf_op jit(solution)/shard_map/ppermute | solution.py:418
  315.9 47.3 %collective-permute-start.30 = (bf16[256,2048]{1,0:T(8,128)(2,1)}, bf16[256,2048]{1,0:T(8,128)(2,1)}, u32[]{:S(2)}, u32[]{:S(2)}) collective-permute-start(bf16[256,2048]{1,0:T(8,128)(2,1)} %bitcast.73), channel_id=1, source_target_pairs={{0,16},{16,0},{8,24},{24,8},{1,17},{17,1},{9,25},{25,9},{2,18},{18... | collective-permute-start | bytes 3145736 | tf_op jit(solution)/shard_map/ppermute | solution.py:414
  340.7 44.8 %collective-permute-start.31 = (bf16[256,2048]{1,0:T(8,128)(2,1)S(1)}, bf16[256,2048]{1,0:T(8,128)(2,1)S(1)}, u32[]{:S(2)}, u32[]{:S(2)}) collective-permute-start(bf16[256,2048]{1,0:T(8,128)(2,1)S(1)} %bitcast.567), channel_id=1, source_target_pairs={{0,16},{16,0},{8,24},{24,8},{1,17},{17,1},{9,25},{25,9},{2,18},{18... | collective-permute-start | bytes 3145736 | tf_op jit(solution)/shard_map/ppermute | solution.py:414
  363.2 44.8 %collective-permute-start.32 = (bf16[256,2048]{1,0:T(8,128)(2,1)S(1)}, bf16[256,2048]{1,0:T(8,128)(2,1)S(1)}, u32[]{:S(2)}, u32[]{:S(2)}) collective-permute-start(bf16[256,2048]{1,0:T(8,128)(2,1)S(1)} %bitcast.565), channel_id=1, source_target_pairs={{0,16},{16,0},{8,24},{24,8},{1,17},{17,1},{9,25},{25,9},{2,18},{18... | collective-permute-start | bytes 3145736 | tf_op jit(solution)/shard_map/ppermute | solution.py:414
  379.4 97.6 %collective-permute-start.28 = (bf16[512,2048]{1,0:T(8,128)(2,1)}, bf16[512,2048]{1,0:T(8,128)(2,1)}, u32[]{:S(2)}, u32[]{:S(2)}) collective-permute-start(bf16[512,2048]{1,0:T(8,128)(2,1)} %multiply_convert_fusion), channel_id=1, source_target_pairs={{0,4},{4,0},{1,5},{5,1},{2,6},{6,2},{3,7},{7,3},{8,12},{12,8},{9,1... | collective-permute-start | bytes 6291464 | tf_op jit(solution)/shard_map/ppermute | solution.py:418
  385.6 45.0 %collective-permute-start.33 = (bf16[256,2048]{1,0:T(8,128)(2,1)S(1)}, bf16[256,2048]{1,0:T(8,128)(2,1)}, u32[]{:S(2)}, u32[]{:S(2)}) collective-permute-start(bf16[256,2048]{1,0:T(8,128)(2,1)S(1)} %bitcast.563), channel_id=1, source_target_pairs={{0,16},{16,0},{8,24},{24,8},{1,17},{17,1},{9,25},{25,9},{2,18},{18... | collective-permute-start | bytes 3145736 | tf_op jit(solution)/shard_map/ppermute | solution.py:414
  409.0 44.1 %collective-permute-start.34 = (bf16[256,2048]{1,0:T(8,128)(2,1)S(1)}, bf16[256,2048]{1,0:T(8,128)(2,1)}, u32[]{:S(2)}, u32[]{:S(2)}) collective-permute-start(bf16[256,2048]{1,0:T(8,128)(2,1)S(1)} %bitcast.561), channel_id=1, source_target_pairs={{0,16},{16,0},{8,24},{24,8},{1,17},{17,1},{9,25},{25,9},{2,18},{18... | collective-permute-start | bytes 3145736 | tf_op jit(solution)/shard_map/ppermute | solution.py:414
  430.6 33.7 %collective-permute-start.37 = (bf16[256,1024]{1,0:T(8,128)(2,1)}, bf16[256,1024]{1,0:T(8,128)(2,1)}, u32[]{:S(2)}, u32[]{:S(2)}) collective-permute-start(bf16[256,1024]{1,0:T(8,128)(2,1)} %bitcast.80), channel_id=1, source_target_pairs={{0,16},{16,0},{8,24},{24,8},{1,17},{17,1},{9,25},{25,9},{2,18},{18... | collective-permute-start | bytes 1572872 | tf_op jit(solution)/shard_map/ppermute | solution.py:414
  454.5 533.9 %reduce-scatter.7.cloned.1.call-start = ((), (), s32[]{:S(2)}) async-start(), calls=%async_computation.6 | async-start | bytes 5242880 | tf_op jit(solution)/shard_map/reduce_scatter | solution.py:486
  462.2 62.1 %collective-permute-start.35 = (bf16[512,2048]{1,0:T(8,128)(2,1)}, bf16[512,2048]{1,0:T(8,128)(2,1)}, u32[]{:S(2)}, u32[]{:S(2)}) collective-permute-start(bf16[512,2048]{1,0:T(8,128)(2,1)} %multiply_convert_fusion), channel_id=1, source_target_pairs={{0,8},{8,0},{16,24},{24,16},{1,9},{9,1},{17,25},{25,17},{2,10},{10... | collective-permute-start | bytes 6291464 | tf_op jit(solution)/shard_map/ppermute | solution.py:410
  464.3 81.2 %collective-permute-start.39 = (bf16[256,1024]{1,0:T(8,128)(2,1)}, bf16[256,1024]{1,0:T(8,128)(2,1)}, u32[]{:S(2)}, u32[]{:S(2)}) collective-permute-start(bf16[256,1024]{1,0:T(8,128)(2,1)} %bitcast.91), channel_id=1, source_target_pairs={{0,16},{16,0},{8,24},{24,8},{1,17},{17,1},{9,25},{25,9},{2,18},{18... | collective-permute-start | bytes 1572872 | tf_op jit(solution)/shard_map/ppermute | solution.py:414
  475.6 71.8 %collective-permute-start.40 = (bf16[256,1024]{1,0:T(8,128)(2,1)}, bf16[256,1024]{1,0:T(8,128)(2,1)}, u32[]{:S(2)}, u32[]{:S(2)}) collective-permute-start(bf16[256,1024]{1,0:T(8,128)(2,1)} %bitcast.92), channel_id=1, source_target_pairs={{0,16},{16,0},{8,24},{24,8},{1,17},{17,1},{9,25},{25,9},{2,18},{18... | collective-permute-start | bytes 1572872 | tf_op jit(solution)/shard_map/ppermute | solution.py:414
  524.3 33.6 %collective-permute-start.36 = (bf16[512,2048]{1,0:T(8,128)(2,1)}, bf16[512,2048]{1,0:T(8,128)(2,1)S(1)}, u32[]{:S(2)}, u32[]{:S(2)}) collective-permute-start(bf16[512,2048]{1,0:T(8,128)(2,1)} %collective-permute-done.35), channel_id=1, source_target_pairs={{0,4},{4,0},{1,5},{5,1},{2,6},{6,2},{3,7},{7,3},{8,12},{12,8},{9,1... | collective-permute-start | bytes 6291464 | tf_op jit(solution)/shard_map/ppermute | solution.py:418
  610.9 47.9 %collective-permute-start.43 = (bf16[512,2048]{1,0:T(8,128)(2,1)S(1)}, bf16[512,2048]{1,0:T(8,128)(2,1)S(1)}, u32[]{:S(2)}, u32[]{:S(2)}) collective-permute-start(bf16[512,2048]{1,0:T(8,128)(2,1)S(1)} %add_convert_fusion.12), channel_id=1, source_target_pairs={{0,8},{8,0},{16,24},{24,16},{1,9},{9,1},{17,25},{25,17},{2,10},{10... | collective-permute-start | bytes 6291464 | tf_op jit(solution)/shard_map/ppermute | solution.py:410
  682.4 48.3 %collective-permute-start.45 = (bf16[512,2048]{1,0:T(8,128)(2,1)}, bf16[512,2048]{1,0:T(8,128)(2,1)}, u32[]{:S(2)}, u32[]{:S(2)}) collective-permute-start(bf16[512,2048]{1,0:T(8,128)(2,1)} %fusion.52), channel_id=1, source_target_pairs={{0,8},{8,0},{16,24},{24,16},{1,9},{9,1},{17,25},{25,17},{2,10},{10... | collective-permute-start | bytes 6291464 | tf_op jit(solution)/shard_map/ppermute | solution.py:410
  783.5 46.9 %collective-permute-start.53 = (bf16[256,1024]{1,0:T(8,128)(2,1)S(1)}, bf16[256,1024]{1,0:T(8,128)(2,1)S(1)}, u32[]{:S(2)}, u32[]{:S(2)}) collective-permute-start(bf16[256,1024]{1,0:T(8,128)(2,1)S(1)} %get-tuple-element.271), channel_id=1, source_target_pairs={{0,16},{16,0},{8,24},{24,8},{1,17},{17,1},{9,25},{25,9},{2,18},{18... | collective-permute-start | bytes 1572872 | tf_op jit(solution)/shard_map/ppermute | solution.py:414
  794.8 308.6 %reduce-scatter.9.cloned.1.call-start = ((), (), s32[]{:S(2)}) async-start(), calls=%async_computation.7 | async-start | bytes 2621440 | tf_op jit(solution)/shard_map/reduce_scatter | solution.py:486
  830.4 62.8 %collective-permute-start.54 = (bf16[256,1024]{1,0:T(8,128)(2,1)}, bf16[256,1024]{1,0:T(8,128)(2,1)}, u32[]{:S(2)}, u32[]{:S(2)}) collective-permute-start(bf16[256,1024]{1,0:T(8,128)(2,1)} %get-tuple-element.137), channel_id=1, source_target_pairs={{0,16},{16,0},{8,24},{24,8},{1,17},{17,1},{9,25},{25,9},{2,18},{18... | collective-permute-start | bytes 1572872 | tf_op jit(solution)/shard_map/ppermute | solution.py:414
  832.0 62.8 %collective-permute-start.49 = (bf16[256,1024]{1,0:T(8,128)(2,1)}, bf16[256,1024]{1,0:T(8,128)(2,1)}, u32[]{:S(2)}, u32[]{:S(2)}) collective-permute-start(bf16[256,1024]{1,0:T(8,128)(2,1)} %get-tuple-element.133), channel_id=1, source_target_pairs={{0,16},{16,0},{8,24},{24,8},{1,17},{17,1},{9,25},{25,9},{2,18},{18... | collective-permute-start | bytes 1572872 | tf_op jit(solution)/shard_map/ppermute | solution.py:414
  842.6 112.4 %collective-permute-start.48 = (bf16[512,2048]{1,0:T(8,128)(2,1)}, bf16[512,2048]{1,0:T(8,128)(2,1)S(1)}, u32[]{:S(2)}, u32[]{:S(2)}) collective-permute-start(bf16[512,2048]{1,0:T(8,128)(2,1)} %add_convert_fusion.9), channel_id=1, source_target_pairs={{0,4},{4,0},{1,5},{5,1},{2,6},{6,2},{3,7},{7,3},{8,12},{12,8},{9,1... | collective-permute-start | bytes 6291464 | tf_op jit(solution)/shard_map/ppermute | solution.py:418
  894.8 47.2 %collective-permute-start.50 = (bf16[256,2048]{1,0:T(8,128)(2,1)S(1)}, bf16[256,2048]{1,0:T(8,128)(2,1)}, u32[]{:S(2)}, u32[]{:S(2)}) collective-permute-start(bf16[256,2048]{1,0:T(8,128)(2,1)S(1)} %get-tuple-element.134), channel_id=1, source_target_pairs={{0,16},{16,0},{8,24},{24,8},{1,17},{17,1},{9,25},{25,9},{2,18},{18... | collective-permute-start | bytes 3145736 | tf_op jit(solution)/shard_map/ppermute | solution.py:414
  904.7 302.4 %reduce-scatter.17.cloned.1.call-start = ((), (), s32[]{:S(2)}) async-start(), calls=%async_computation.11 | async-start | bytes 5242880 | tf_op jit(solution)/shard_map/reduce_scatter | solution.py:486
  919.5 44.9 %collective-permute-start.57 = (bf16[256,2048]{1,0:T(8,128)(2,1)}, bf16[256,2048]{1,0:T(8,128)(2,1)}, u32[]{:S(2)}, u32[]{:S(2)}) collective-permute-start(bf16[256,2048]{1,0:T(8,128)(2,1)} %get-tuple-element.141), channel_id=1, source_target_pairs={{0,16},{16,0},{8,24},{24,8},{1,17},{17,1},{9,25},{25,9},{2,18},{18... | collective-permute-start | bytes 3145736 | tf_op jit(solution)/shard_map/ppermute | solution.py:414
  942.0 44.9 %collective-permute-start.56 = (bf16[256,2048]{1,0:T(8,128)(2,1)}, bf16[256,2048]{1,0:T(8,128)(2,1)}, u32[]{:S(2)}, u32[]{:S(2)}) collective-permute-start(bf16[256,2048]{1,0:T(8,128)(2,1)} %get-tuple-element.140), channel_id=1, source_target_pairs={{0,16},{16,0},{8,24},{24,8},{1,17},{17,1},{9,25},{25,9},{2,18},{18... | collective-permute-start | bytes 3145736 | tf_op jit(solution)/shard_map/ppermute | solution.py:414
  957.5 75.9 %collective-permute-start.52 = (bf16[512,2048]{1,0:T(8,128)(2,1)}, bf16[512,2048]{1,0:T(8,128)(2,1)S(1)}, u32[]{:S(2)}, u32[]{:S(2)}) collective-permute-start(bf16[512,2048]{1,0:T(8,128)(2,1)} %add_convert_fusion.8), channel_id=1, source_target_pairs={{0,8},{8,0},{16,24},{24,16},{1,9},{9,1},{17,25},{25,17},{2,10},{10... | collective-permute-start | bytes 6291464 | tf_op jit(solution)/shard_map/ppermute | solution.py:410
  964.4 46.6 %collective-permute-start.59 = (bf16[256,2048]{1,0:T(8,128)(2,1)}, bf16[256,2048]{1,0:T(8,128)(2,1)}, u32[]{:S(2)}, u32[]{:S(2)}) collective-permute-start(bf16[256,2048]{1,0:T(8,128)(2,1)} %get-tuple-element.143), channel_id=1, source_target_pairs={{0,16},{16,0},{8,24},{24,8},{1,17},{17,1},{9,25},{25,9},{2,18},{18... | collective-permute-start | bytes 3145736 | tf_op jit(solution)/shard_map/ppermute | solution.py:414
  986.9 44.9 %collective-permute-start.69 = (bf16[256,2048]{1,0:T(8,128)(2,1)}, bf16[256,2048]{1,0:T(8,128)(2,1)}, u32[]{:S(2)}, u32[]{:S(2)}) collective-permute-start(bf16[256,2048]{1,0:T(8,128)(2,1)} %get-tuple-element.151), channel_id=1, source_target_pairs={{0,16},{16,0},{8,24},{24,8},{1,17},{17,1},{9,25},{25,9},{2,18},{18... | collective-permute-start | bytes 3145736 | tf_op jit(solution)/shard_map/ppermute | solution.py:414
  999.6 44.5 %collective-permute-start.51 = (bf16[512,2048]{1,0:T(8,128)(2,1)}, bf16[512,2048]{1,0:T(8,128)(2,1)}, u32[]{:S(2)}, u32[]{:S(2)}) collective-permute-start(bf16[512,2048]{1,0:T(8,128)(2,1)} %add_convert_fusion.7), channel_id=1, source_target_pairs={{0,4},{4,0},{1,5},{5,1},{2,6},{6,2},{3,7},{7,3},{8,12},{12,8},{9,1... | collective-permute-start | bytes 6291464 | tf_op jit(solution)/shard_map/ppermute | solution.py:418
  1010.9 229.2 %reduce-scatter.13.cloned.1.call-start = ((), (), s32[]{:S(2)}) async-start(), calls=%async_computation.9 | async-start | bytes 5242880 | tf_op jit(solution)/shard_map/reduce_scatter | solution.py:486
  1011.0 61.3 %collective-permute-start.71 = (bf16[256,2048]{1,0:T(8,128)(2,1)}, bf16[256,2048]{1,0:T(8,128)(2,1)}, u32[]{:S(2)}, u32[]{:S(2)}) collective-permute-start(bf16[256,2048]{1,0:T(8,128)(2,1)} %get-tuple-element.153), channel_id=1, source_target_pairs={{0,16},{16,0},{8,24},{24,8},{1,17},{17,1},{9,25},{25,9},{2,18},{18... | collective-permute-start | bytes 3145736 | tf_op jit(solution)/shard_map/ppermute | solution.py:414
  1031.8 44.6 %collective-permute-start.70 = (bf16[256,2048]{1,0:T(8,128)(2,1)}, bf16[256,2048]{1,0:T(8,128)(2,1)}, u32[]{:S(2)}, u32[]{:S(2)}) collective-permute-start(bf16[256,2048]{1,0:T(8,128)(2,1)} %get-tuple-element.152), channel_id=1, source_target_pairs={{0,16},{16,0},{8,24},{24,8},{1,17},{17,1},{9,25},{25,9},{2,18},{18... | collective-permute-start | bytes 3145736 | tf_op jit(solution)/shard_map/ppermute | solution.py:414
  1087.3 300.7 %reduce-scatter.15.cloned.1.call-start = ((), (), s32[]{:S(2)}) async-start(), calls=%async_computation.10 | async-start | bytes 1310720 | tf_op jit(solution)/shard_map/reduce_scatter | solution.py:486
  1094.0 107.6 %collective-permute-start.79 = (bf16[2,512,384]{2,1,0:T(8,128)(2,1)}, bf16[2,512,384]{2,1,0:T(8,128)(2,1)}, u32[]{:S(2)}, u32[]{:S(2)}) collective-permute-start(bf16[2,512,384]{2,1,0:T(8,128)(2,1)} %dynamic-slice_bitcast_fusion), channel_id=1, source_target_pairs={{0,8},{8,0},{16,24},{24,16},{1,9},{9,1},{17,25},{25,17},{2,10},{10... | collective-permute-start | bytes 2359304 | tf_op jit(solution)/shard_map/ppermute | solution.py:410
  1172.4 34.7 %collective-permute-start.89 = (bf16[4,64,1024]{2,1,0:T(8,128)(2,1)}, bf16[4,64,1024]{2,1,0:T(8,128)(2,1)}, u32[]{:S(2)}, u32[]{:S(2)}) collective-permute-start(bf16[4,64,1024]{2,1,0:T(8,128)(2,1)} %bitcast.162), channel_id=1, source_target_pairs={{0,16},{16,0},{8,24},{24,8},{1,17},{17,1},{9,25},{25,9},{2,18},{18... | collective-permute-start | bytes 1572872 | tf_op jit(solution)/shard_map/ppermute | solution.py:414
  1226.2 28.0 %collective-permute-start.72 = (bf16[256,1024]{1,0:T(8,128)(2,1)}, bf16[256,1024]{1,0:T(8,128)(2,1)}, u32[]{:S(2)}, u32[]{:S(2)}) collective-permute-start(bf16[256,1024]{1,0:T(8,128)(2,1)} %get-tuple-element.155), channel_id=1, source_target_pairs={{0,16},{16,0},{8,24},{24,8},{1,17},{17,1},{9,25},{25,9},{2,18},{18... | collective-permute-start | bytes 1572872 | tf_op jit(solution)/shard_map/ppermute | solution.py:414
  1226.7 27.6 %collective-permute-start.74 = (bf16[256,1024]{1,0:T(8,128)(2,1)}, bf16[256,1024]{1,0:T(8,128)(2,1)}, u32[]{:S(2)}, u32[]{:S(2)}) collective-permute-start(bf16[256,1024]{1,0:T(8,128)(2,1)} %get-tuple-element.157), channel_id=1, source_target_pairs={{0,16},{16,0},{8,24},{24,8},{1,17},{17,1},{9,25},{25,9},{2,18},{18... | collective-permute-start | bytes 1572872 | tf_op jit(solution)/shard_map/ppermute | solution.py:414
  1228.3 33.2 %collective-permute-start.66 = (bf16[256,1024]{1,0:T(8,128)(2,1)}, bf16[256,1024]{1,0:T(8,128)(2,1)}, u32[]{:S(2)}, u32[]{:S(2)}) collective-permute-start(bf16[256,1024]{1,0:T(8,128)(2,1)} %get-tuple-element.148), channel_id=1, source_target_pairs={{0,8},{8,0},{16,24},{24,16},{1,9},{9,1},{17,25},{25,17},{2,10},{10... | collective-permute-start | bytes 1572872 | tf_op jit(solution)/shard_map/ppermute | solution.py:410
  1238.9 33.8 %collective-permute-start.62 = (bf16[256,1024]{1,0:T(8,128)(2,1)}, bf16[256,1024]{1,0:T(8,128)(2,1)}, u32[]{:S(2)}, u32[]{:S(2)}) collective-permute-start(bf16[256,1024]{1,0:T(8,128)(2,1)} %get-tuple-element.145), channel_id=1, source_target_pairs={{0,8},{8,0},{16,24},{24,16},{1,9},{9,1},{17,25},{25,17},{2,10},{10... | collective-permute-start | bytes 1572872 | tf_op jit(solution)/shard_map/ppermute | solution.py:410
  1250.3 33.7 %collective-permute-start.87 = (bf16[2,64,2048]{2,1,0:T(8,128)(2,1)}, bf16[2,64,2048]{2,1,0:T(8,128)(2,1)}, u32[]{:S(2)}, u32[]{:S(2)}) collective-permute-start(bf16[2,64,2048]{2,1,0:T(8,128)(2,1)} %dynamic-slice_bitcast_fusion.1), channel_id=1, source_target_pairs={{0,8},{8,0},{16,24},{24,16},{1,9},{9,1},{17,25},{25,17},{2,10},{10... | collective-permute-start | bytes 1572872 | tf_op jit(solution)/shard_map/ppermute | solution.py:410
  1254.2 69.4 %collective-permute-start.60 = (bf16[512,2048]{1,0:T(8,128)(2,1)}, bf16[512,2048]{1,0:T(8,128)(2,1)}, u32[]{:S(2)}, u32[]{:S(2)}) collective-permute-start(bf16[512,2048]{1,0:T(8,128)(2,1)} %add_convert_fusion.5), channel_id=1, source_target_pairs={{0,4},{4,0},{1,5},{5,1},{2,6},{6,2},{3,7},{7,3},{8,12},{12,8},{9,1... | collective-permute-start | bytes 6291464 | tf_op jit(solution)/shard_map/ppermute | solution.py:418
  1254.3 32.6 %collective-permute-start.91 = (bf16[2,64,2048]{2,1,0:T(8,128)(2,1)}, bf16[2,64,2048]{2,1,0:T(8,128)(2,1)S(1)}, u32[]{:S(2)}, u32[]{:S(2)}) collective-permute-start(bf16[2,64,2048]{2,1,0:T(8,128)(2,1)} %pad_maximum_fusion.35), channel_id=1, source_target_pairs={{0,4},{4,0},{1,5},{5,1},{2,6},{6,2},{3,7},{7,3},{8,12},{12,8},{9,1... | collective-permute-start | bytes 1572872 | tf_op jit(solution)/shard_map/ppermute | solution.py:418
  1261.5 27.1 %collective-permute-start.86 = (bf16[2,64,2048]{2,1,0:T(8,128)(2,1)}, bf16[2,64,2048]{2,1,0:T(8,128)(2,1)}, u32[]{:S(2)}, u32[]{:S(2)}) collective-permute-start(bf16[2,64,2048]{2,1,0:T(8,128)(2,1)} %pad_maximum_fusion.33), channel_id=1, source_target_pairs={{0,4},{4,0},{1,5},{5,1},{2,6},{6,2},{3,7},{7,3},{8,12},{12,8},{9,1... | collective-permute-start | bytes 1572872 | tf_op jit(solution)/shard_map/ppermute | solution.py:418
  1277.1 127.4 %reduce-scatter.11.cloned.1.call-start = ((), (), s32[]{:S(2)}) async-start(), calls=%async_computation.8 | async-start | bytes 1966080 | tf_op jit(solution)/shard_map/reduce_scatter | solution.py:486
  1284.0 33.6 %collective-permute-start.63 = (bf16[256,1536]{1,0:T(8,128)(2,1)}, bf16[256,1536]{1,0:T(8,128)(2,1)S(1)}, u32[]{:S(2)}, u32[]{:S(2)}) collective-permute-start(bf16[256,1536]{1,0:T(8,128)(2,1)} %get-tuple-element.146), channel_id=1, source_target_pairs={{0,8},{8,0},{16,24},{24,16},{1,9},{9,1},{17,25},{25,17},{2,10},{10... | collective-permute-start | bytes 2359304 | tf_op jit(solution)/shard_map/ppermute | solution.py:410
  1286.9 49.1 %collective-permute-start.88 = (bf16[2,64,2048]{2,1,0:T(8,128)(2,1)}, bf16[2,64,2048]{2,1,0:T(8,128)(2,1)}, u32[]{:S(2)}, u32[]{:S(2)}) collective-permute-start(bf16[2,64,2048]{2,1,0:T(8,128)(2,1)} %pad_maximum_fusion.34), channel_id=1, source_target_pairs={{0,4},{4,0},{1,5},{5,1},{2,6},{6,2},{3,7},{7,3},{8,12},{12,8},{9,1... | collective-permute-start | bytes 1572872 | tf_op jit(solution)/shard_map/ppermute | solution.py:418
  1300.7 59.2 %collective-permute-start.68 = (bf16[256,1536]{1,0:T(8,128)(2,1)}, bf16[256,1536]{1,0:T(8,128)(2,1)}, u32[]{:S(2)}, u32[]{:S(2)}) collective-permute-start(bf16[256,1536]{1,0:T(8,128)(2,1)} %get-tuple-element.150), channel_id=1, source_target_pairs={{0,8},{8,0},{16,24},{24,16},{1,9},{9,1},{17,25},{25,17},{2,10},{10... | collective-permute-start | bytes 2359304 | tf_op jit(solution)/shard_map/ppermute | solution.py:410
  1317.6 33.4 %collective-permute-start.64 = (bf16[256,1536]{1,0:T(8,128)(2,1)}, bf16[256,1536]{1,0:T(8,128)(2,1)}, u32[]{:S(2)}, u32[]{:S(2)}) collective-permute-start(bf16[256,1536]{1,0:T(8,128)(2,1)} %get-tuple-element.147), channel_id=1, source_target_pairs={{0,8},{8,0},{16,24},{24,16},{1,9},{9,1},{17,25},{25,17},{2,10},{10... | collective-permute-start | bytes 2359304 | tf_op jit(solution)/shard_map/ppermute | solution.py:410
  1323.1 38.0 %collective-permute-start.75 = (bf16[256,1536]{1,0:T(8,128)(2,1)}, bf16[256,1536]{1,0:T(8,128)(2,1)}, u32[]{:S(2)}, u32[]{:S(2)}) collective-permute-start(bf16[256,1536]{1,0:T(8,128)(2,1)} %get-tuple-element.158), channel_id=1, source_target_pairs={{0,16},{16,0},{8,24},{24,8},{1,17},{17,1},{9,25},{25,9},{2,18},{18... | collective-permute-start | bytes 2359304 | tf_op jit(solution)/shard_map/ppermute | solution.py:414
  1323.6 35.1 %collective-permute-start.73 = (bf16[256,1536]{1,0:T(8,128)(2,1)}, bf16[256,1536]{1,0:T(8,128)(2,1)}, u32[]{:S(2)}, u32[]{:S(2)}) collective-permute-start(bf16[256,1536]{1,0:T(8,128)(2,1)} %get-tuple-element.156), channel_id=1, source_target_pairs={{0,16},{16,0},{8,24},{24,8},{1,17},{17,1},{9,25},{25,9},{2,18},{18... | collective-permute-start | bytes 2359304 | tf_op jit(solution)/shard_map/ppermute | solution.py:414
  1336.1 30.2 %collective-permute-start.92 = (f32[8,2048]{1,0:T(8,128)S(1)}, f32[8,2048]{1,0:T(8,128)S(1)}, u32[]{:S(2)}, u32[]{:S(2)}) collective-permute-start(f32[8,2048]{1,0:T(8,128)S(1)} %pad_maximum_fusion.40), channel_id=1, source_target_pairs={{0,4},{4,0},{1,5},{5,1},{2,6},{6,2},{3,7},{7,3},{8,12},{12,8},{9,1... | collective-permute-start | bytes 196616 | tf_op jit(solution)/shard_map/ppermute | solution.py:418
  (270 other events, 4882.9 us)
Sparse Core Ops, SparseCore 0:
  16.0 46.1 all-gather.14
  63.7 32.8 all-gather.12
  98.8 79.5 all-gather.16
  179.8 79.2 all-gather.18
  260.6 44.4 all-gather.20
  454.6 84.1 all-gather.22
  795.0 75.2 reduce-scatter.6
  904.9 41.7 reduce-scatter.8
  1011.0 74.5 reduce-scatter.16
  1087.9 77.2 reduce-scatter.12
  1277.2 25.8 reduce-scatter.14
  1366.4 38.0 reduce-scatter.10

commit v2 on v1

--- a/solution.py
+++ b/solution.py
@@ -909,7 +909,7 @@
     out_near = chained(swap_x, out_sent[2:] + out_sent[:2])
     out_near = out_near[2:] + out_near[:2]
     d_heads = project(d_attn_pairs, output_w)
-    d_heads = after(d_heads, (up_near[1], down_four))
+    d_heads = after(d_heads, (up_near[1], down_four, out_near[2:]))
     d_query_low, d_key_low, d_value_low, d_query_g, d_key_g = attend_back(
         d_heads,
         query_raw,
@@ -926,6 +926,9 @@
         score_scale,
     )
 
+    up_kept = ff_keep(up_sides, [after(up_near[0], d_heads)] + up_near[1:])
+    up_four = scatter_z(up_kept)
+    d_query_low = after(d_query_low, (out_near[:2], up_kept))
     d_query_low, d_key_low, d_value_low = [
         entry.astype(BF16) for entry in (d_query_low, d_key_low, d_value_low)
     ]
@@ -938,8 +941,6 @@
     first_sent = pair_send(first_sides)
     first_near = chained(swap_x, first_sent[2:] + first_sent[:2], out_near[:2])
     first_near = first_near[2:] + first_near[:2]
-    up_kept = ff_keep(up_sides, up_near)
-    up_four = scatter_z(up_kept)
     small_halves = small_sums(
         [x_low, d_laurel_low, second_low, d_plproj_low],
         [d_left_low, left_low, d_plgate_low, gated_low],
@@ -989,14 +990,14 @@
         whole_columns(small_keep, swap_core(small_send)), [rank, rank, pl_width, pl_width]
     )
 
-    down_eight, down_four = after((down_eight, down_four), d_query_low)
+    down_eight, down_four = after((down_eight, down_four), first_near)
     down_eight = down_eight.reshape(2, 4, rows, ff_half)
     down_last = down_eight[0].astype(f32) + swap_y(down_eight[1]).astype(f32)
     grad_down = ff_owned(
         jnp.concatenate([down_last.astype(BF16), down_four.reshape(4, rows, ff_half)], 2)
     )
-    grad_gate = ff_owned(after(gate_four, out_passed))
-    grad_up = ff_owned(up_four)
+    grad_gate = ff_owned(after(gate_four, first_near))
+    grad_up = ff_owned(after(up_four, first_near))
 
     gain_grads = jnp.stack(
         [d_input_g, d_attn_g, d_laurel_g, d_preffw_g, d_ffw_g, d_perlayer_g]

time: 1420 us -> 1410 us (level)
  waiting for transfers between devices: 520 us -> 501 us
  matrix products: 430 us -> 446 us
    ppermute x25, waiting for transfers between devices: 198 us -> 181 us  [swap_x(): return lax.ppermute(array, 'batch', X_PAIRS)]
    unnamed x504 -> x526, local copies, waits for them, and re-layouts: 93.4 us -> 82.6 us
  transfers between devices with their start and end apart: 110 -> 110, of which waited for: 52 -> 51; matrix products, arithmetic and copies ran while one was open for 45% -> 48% of each run, Pallas kernels for 0% -> 0%
where the time goes in v2:
time: 1410 us; the launch traced here: 1400 us
  waiting for transfers between devices  501 us (36%)
  matrix products  446 us (32%)
  local copies, waits for them, and re-layouts  188 us (13%)
  other arithmetic  158 us (11%)
  starting transfers between devices  92.7 us (7%)
  between operations  18.1 us (1%)
    ppermute x37, waiting for transfers between devices, swap_y(): return lax.ppermute(array, 'batch', Y_PAIRS)  255 us
    ppermute x25, waiting for transfers between devices, swap_x(): return lax.ppermute(array, 'batch', X_PAIRS)  181 us
    dot_general x24, matrix products, against_rows(): lax.dot_general(left, right, (((1,), (1,)), ((), ())), preferred_element_...  151 us
    dot_general x30, matrix products, over_tokens(): lax.dot_general(left, right, (((0,), (0,)), ((), ())), preferred_element_...  132 us
    dot_general x14, matrix products, project(): return jnp.dot(left, right, preferred_element_type=jnp.float32)  114 us
    unnamed x526, local copies, waits for them, and re-layouts  82.6 us
    ppermute x37, starting transfers between devices, swap_y(): return lax.ppermute(array, 'batch', Y_PAIRS)  44.1 us
    ppermute x25, starting transfers between devices, swap_x(): return lax.ppermute(array, 'batch', X_PAIRS)  32.5 us
  transfers between devices with their start and end apart: 110, of which 51 were waited for; matrix products, arithmetic and copies ran while one was open for 48% of the time, Pallas kernels for 0%

profile of v2, /device:TPU:0, one launch (start us, length us, event | category | flops | bytes accessed | tf_op | source)
XLA Modules:
  0.0 1404.2 jit_solution(16818188679249512553)
XLA Ops:
  29.4 10.3 collective-permute-done.2
  63.2 13.6 collective-permute-done.4
  89.0 8.1 collective-permute-done.7
  101.9 10.4 collective-permute-done.14
  116.4 9.3 collective-permute-done.15
  149.8 23.0 %collective-permute-done.17 = bf16[512,1920]{1,0:T(8,128)(2,1)} collective-permute-done((bf16[512,1920]{1,0:T(8,128)(2,1)}, bf16[512,1920]{1,0:T(8,128)(2,1)}, u32[]{:S(2)}, u32[]{:S(2)}) %collective-permute-start.17) | collective-permute-done | bytes 1966112 | tf_op jit(solution)/shard_map/ppermute | solution.py:410
  186.4 9.2 collective-permute-done.18
  225.3 34.4 %collective-permute-done.22 = bf16[256,2048]{1,0:T(8,128)(2,1)} collective-permute-done((bf16[256,2048]{1,0:T(8,128)(2,1)S(1)}, bf16[256,2048]{1,0:T(8,128)(2,1)}, u32[]{:S(2)}, u32[]{:S(2)}) %collective-permute-start.22) | collective-permute-done | bytes 1048608 | tf_op jit(solution)/shard_map/ppermute | solution.py:414
  275.6 7.9 fusion.342
  283.5 8.1 exponential_reduce_fusion
  291.6 8.6 fusion.79
  328.4 17.5 %collective-permute-done.29 = bf16[256,2048]{1,0:T(8,128)(2,1)S(1)} collective-permute-done((bf16[256,2048]{1,0:T(8,128)(2,1)}, bf16[256,2048]{1,0:T(8,128)(2,1)S(1)}, u32[]{:S(2)}, u32[]{:S(2)}) %collective-permute-start.29) | collective-permute-done | bytes 1048608 | tf_op jit(solution)/shard_map/ppermute | solution.py:414
  347.4 21.1 %collective-permute-done.30 = bf16[256,2048]{1,0:T(8,128)(2,1)} collective-permute-done((bf16[256,2048]{1,0:T(8,128)(2,1)}, bf16[256,2048]{1,0:T(8,128)(2,1)}, u32[]{:S(2)}, u32[]{:S(2)}) %collective-permute-start.30) | collective-permute-done | bytes 1048608 | tf_op jit(solution)/shard_map/ppermute | solution.py:414
  392.3 21.0 %collective-permute-done.32 = bf16[256,2048]{1,0:T(8,128)(2,1)S(1)} collective-permute-done((bf16[256,2048]{1,0:T(8,128)(2,1)S(1)}, bf16[256,2048]{1,0:T(8,128)(2,1)S(1)}, u32[]{:S(2)}, u32[]{:S(2)}) %collective-permute-start.32) | collective-permute-done | bytes 1048608 | tf_op jit(solution)/shard_map/ppermute | solution.py:414
  418.6 17.3 %collective-permute-done.33 = bf16[256,2048]{1,0:T(8,128)(2,1)} collective-permute-done((bf16[256,2048]{1,0:T(8,128)(2,1)}, bf16[256,2048]{1,0:T(8,128)(2,1)}, u32[]{:S(2)}, u32[]{:S(2)}) %collective-permute-start.33) | collective-permute-done | bytes 1048608 | tf_op jit(solution)/shard_map/ppermute | solution.py:414
  437.3 21.0 %collective-permute-done.34 = bf16[256,2048]{1,0:T(8,128)(2,1)} collective-permute-done((bf16[256,2048]{1,0:T(8,128)(2,1)S(1)}, bf16[256,2048]{1,0:T(8,128)(2,1)}, u32[]{:S(2)}, u32[]{:S(2)}) %collective-permute-start.34) | collective-permute-done | bytes 1048608 | tf_op jit(solution)/shard_map/ppermute | solution.py:414
  471.1 9.8 collective-permute-done.38
  496.8 14.8 %fusion.318 = f32[1024,2048]{1,0:T(8,128)} fusion(bf16[2048,2048]{1,0:T(8,128)(2,1)S(1)} %constant_dynamic-update-slice_fusion.10, bf16[512,2048]{1,0:T(8,128)(2,1)} %collective-permute-done.28, bf16[512,2048]{1,0:T(8,128)(2,1)} %multiply_convert_fusion), kind=kOutput, calls=%fused_computation.690 | convolution fusion | flops 8598323200 | bytes 20971520 | tf_op jit(solution)/shard_map/dot_general | solution.py:78
  511.7 16.5 %fusion.20 = (bf16[1024,2048]{1,0:T(8,128)(2,1)}, bf16[1024,2048]{1,0:T(8,128)(2,1)}) fusion(f32[1024,2048]{1,0:T(8,128)} %fusion.318, bf16[2048,2048]{1,0:T(8,128)(2,1)S(1)} %constant_dynamic-update-slice_fusion.18, bf16[512,2048]{1,0:T(8,128)(2,1)} %collective-permute-done.28, bf16[512,2048]{1,0:T(8,128)(2,1)} %multiply_convert_fusion), kind=kOutput, calls=%fused_computation.37 | convolution fusion | flops 8621391872 | bytes 29360128 | tf_op jit(solution)/shard_map/dot_general | solution.py:78
  528.3 11.8 all-gather.23.cloned.1.call-done
  560.0 8.9 fusion.343
  568.9 13.1 fusion.323
  582.0 8.7 convolution_convert_fusion.2
  595.0 7.4 add_convert_fusion.12
  603.9 7.4 convolution_convert_fusion.1
  611.4 7.6 fusion.119
  619.0 31.1 %collective-permute-done.43 = bf16[512,2048]{1,0:T(8,128)(2,1)S(1)} collective-permute-done((bf16[512,2048]{1,0:T(8,128)(2,1)S(1)}, bf16[512,2048]{1,0:T(8,128)(2,1)S(1)}, u32[]{:S(2)}, u32[]{:S(2)}) %collective-permute-start.43) | collective-permute-done | bytes 2097184 | tf_op jit(solution)/shard_map/ppermute | solution.py:410
  675.3 22.3 %fusion.36 = (bf16[1024,2048]{1,0:T(8,128)(2,1)}, bf16[1024,2048]{1,0:T(8,128)(2,1)}) fusion(f32[1024,2048]{1,0:T(8,128)} %fusion.318, bf16[1024,2048]{1,0:T(8,128)(2,1)} %get-tuple-element.394, bf16[2048,1024]{1,0:T(8,128)(2,1)} %constant_dynamic-update-slice_fusion.36, bf16[2048,1024]{1,0:T(8,128)(2,1)} %constant_dynamic-update-slice_fusion.28, ...), kind=kOutput, calls=%fused_computation.53 | convolution fusion | flops 8671723520 | bytes 33554432 | tf_op jit(solution)/shard_map/dot_general | solution.py:78
  697.7 24.4 %collective-permute-done.45 = bf16[512,2048]{1,0:T(8,128)(2,1)S(1)} collective-permute-done((bf16[512,2048]{1,0:T(8,128)(2,1)}, bf16[512,2048]{1,0:T(8,128)(2,1)S(1)}, u32[]{:S(2)}, u32[]{:S(2)}) %collective-permute-start.45) | collective-permute-done | bytes 2097184 | tf_op jit(solution)/shard_map/ppermute | solution.py:410
  722.4 9.5 fusion.97
  731.9 9.6 fusion.99
  747.3 13.4 fusion.319
  760.8 7.2 fusion.101
  773.8 8.3 add_convert_fusion.3
  792.3 9.2 fusion.8
  801.5 9.9 fusion.104
  811.4 7.0 fusion.132
  818.4 10.0 add_convert_fusion.9
  828.5 7.0 fusion.130
  838.3 7.2 fusion.109
  845.5 7.3 fusion.107
  852.8 11.9 add_convert_fusion.4
  864.7 12.0 add_convert_fusion.2
  882.9 7.1 fusion.126
  890.0 7.4 fusion.128
  897.3 30.6 %collective-permute-done.55 = bf16[256,2048]{1,0:T(8,128)(2,1)S(1)} collective-permute-done((bf16[256,2048]{1,0:T(8,128)(2,1)S(1)}, bf16[256,2048]{1,0:T(8,128)(2,1)S(1)}, u32[]{:S(2)}, u32[]{:S(2)}) %collective-permute-start.55) | collective-permute-done | bytes 1048608 | tf_op jit(solution)/shard_map/ppermute | solution.py:414
  935.0 11.2 add_convert_fusion.7
  958.8 18.1 %collective-permute-done.56 = bf16[256,2048]{1,0:T(8,128)(2,1)} collective-permute-done((bf16[256,2048]{1,0:T(8,128)(2,1)}, bf16[256,2048]{1,0:T(8,128)(2,1)}, u32[]{:S(2)}, u32[]{:S(2)}) %collective-permute-start.56) | collective-permute-done | bytes 1048608 | tf_op jit(solution)/shard_map/ppermute | solution.py:414
  979.7 10.6 fusion.116
  1011.2 8.3 add_convert_fusion.1
  1042.4 8.3 fusion.50
  1055.2 9.3 collective-permute-done.61
  1065.4 14.3 %fusion = (f32[4,1024]{1,0:T(4,128)S(1)}, f32[1024,1024,4]{1,0,2:T(8,128)}) fusion(f32[4,1024,1024]{1,2,0:T(8,128)} %get-tuple-element.392, f32[4,1024]{1,0:T(4,128)S(1)} %copy-done.117, bf16[1024,256,1]{1,0,2:T(8,128)(2,1)S(1)} %copy-done.121, bf16[128,4,8,256]{3,2,1,0:T(8,128)(2,1)} %bitcast.547), kind=kOutput, calls=%fused_computation.2 | convolution fusion | flops 2160062464 | bytes 36208640 | tf_op jit(solution)/shard_map/thd,sd->hts/dot_general | solution.py:590
  1082.6 10.4 fusion.2
  1093.0 7.2 multiply_bitcast_fusion
  1115.1 8.4 fusion.154
  1123.5 8.4 add_convert_fusion
  1164.9 8.2 collective-permute-done.68
  1174.3 12.8 collective-permute-done.70
  1200.5 12.0 collective-permute-done.73
  1215.4 10.3 collective-permute-done.75
  1301.0 6.9 convert_add_fusion.3
  1367.3 11.6 collective-permute-done.87
  1381.0 11.9 reduce-scatter.15.cloned.1.call-done
  (1006 shorter events, 599.2 us)
Async XLA Ops:
  7.2 119.6 %all-gather.15.cloned.1.call-start = ((), (), s32[]{:S(2)}) async-start(), calls=%async_computation.13 | async-start | bytes 2457600 | tf_op jit(solution)/shard_map/all_gather | solution.py:479
  16.6 159.1 %all-gather.13.cloned.1.call-start = ((), (), s32[]{:S(2)}) async-start(), calls=%async_computation.12 | async-start | bytes 1310720 | tf_op jit(solution)/shard_map/all_gather | solution.py:479
  41.9 171.8 %all-gather.17.cloned.1.call-start = ((), (), s32[]{:S(2)}) async-start(), calls=%async_computation.14 | async-start | bytes 5242880 | tf_op jit(solution)/shard_map/all_gather | solution.py:479
  42.6 282.0 %all-gather.19.cloned.1.call-start = ((), (), s32[]{:S(2)}) async-start(), calls=%async_computation.15 | async-start | bytes 5242880 | tf_op jit(solution)/shard_map/all_gather | solution.py:479
  51.2 45.9 %collective-permute-start.11 = (bf16[64,2,2048]{2,0,1:T(8,128)(2,1)}, bf16[64,2,2048]{2,0,1:T(8,128)(2,1)}, u32[]{:S(2)}, u32[]{:S(2)}) collective-permute-start(bf16[64,2,2048]{2,0,1:T(8,128)(2,1)} %bitcast.510), channel_id=1, source_target_pairs={{0,4},{4,0},{1,5},{5,1},{2,6},{6,2},{3,7},{7,3},{8,12},{12,8},{9,1... | collective-permute-start | bytes 1572872 | tf_op jit(solution)/shard_map/ppermute | solution.py:418
  61.0 25.0 %collective-permute-start.13 = (bf16[2,64,2048]{2,1,0:T(8,128)(2,1)S(1)}, bf16[2,64,2048]{2,1,0:T(8,128)(2,1)S(1)}, u32[]{:S(2)}, u32[]{:S(2)}) collective-permute-start(bf16[2,64,2048]{2,1,0:T(8,128)(2,1)S(1)} %fusion.254), channel_id=1, source_target_pairs={{0,8},{8,0},{16,24},{24,16},{1,9},{9,1},{17,25},{25,17},{2,10},{10... | collective-permute-start | bytes 1572872 | tf_op jit(solution)/shard_map/ppermute | solution.py:410
  87.2 328.6 %all-gather.21.cloned.1.call-start = ((), (), s32[]{:S(2)}) async-start(), calls=%async_computation.16 | async-start | bytes 2621440 | tf_op jit(solution)/shard_map/all_gather | solution.py:479
  116.4 24.3 %collective-permute-start.9 = (bf16[512,2048]{1,0:T(8,128)(2,1)}, bf16[512,2048]{1,0:T(8,128)(2,1)}, u32[]{:S(2)}, u32[]{:S(2)}) collective-permute-start(bf16[512,2048]{1,0:T(8,128)(2,1)} %pad_maximum_fusion.12), channel_id=1, source_target_pairs={{0,4},{4,0},{1,5},{5,1},{2,6},{6,2},{3,7},{7,3},{8,12},{12,8},{9,1... | collective-permute-start | bytes 6291464 | tf_op jit(solution)/shard_map/ppermute | solution.py:418
  130.0 42.7 %collective-permute-start.17 = (bf16[512,1920]{1,0:T(8,128)(2,1)}, bf16[512,1920]{1,0:T(8,128)(2,1)}, u32[]{:S(2)}, u32[]{:S(2)}) collective-permute-start(bf16[512,1920]{1,0:T(8,128)(2,1)} %pad_maximum_fusion.15), channel_id=1, source_target_pairs={{0,8},{8,0},{16,24},{24,16},{1,9},{9,1},{17,25},{25,17},{2,10},{10... | collective-permute-start | bytes 5898248 | tf_op jit(solution)/shard_map/ppermute | solution.py:410
  131.2 46.9 %collective-permute-start.16 = (bf16[512,1920]{1,0:T(8,128)(2,1)}, bf16[512,1920]{1,0:T(8,128)(2,1)}, u32[]{:S(2)}, u32[]{:S(2)}) collective-permute-start(bf16[512,1920]{1,0:T(8,128)(2,1)} %pad_maximum_fusion.15), channel_id=1, source_target_pairs={{0,16},{16,0},{8,24},{24,8},{1,17},{17,1},{9,25},{25,9},{2,18},{18... | collective-permute-start | bytes 5898248 | tf_op jit(solution)/shard_map/ppermute | solution.py:414
  140.5 399.6 %all-gather.23.cloned.1.call-start = ((), (), s32[]{:S(2)}) async-start(), calls=%async_computation.17 | async-start | bytes 5242880 | tf_op jit(solution)/shard_map/all_gather | solution.py:479
  209.3 91.0 %collective-permute-start.20 = (bf16[512,1024]{1,0:T(8,128)(2,1)}, bf16[512,1024]{1,0:T(8,128)(2,1)}, u32[]{:S(2)}, u32[]{:S(2)}) collective-permute-start(bf16[512,1024]{1,0:T(8,128)(2,1)} %pad_maximum_fusion.25), channel_id=1, source_target_pairs={{0,8},{8,0},{16,24},{24,16},{1,9},{9,1},{17,25},{25,17},{2,10},{10... | collective-permute-start | bytes 3145736 | tf_op jit(solution)/shard_map/ppermute | solution.py:410
  210.8 89.5 %collective-permute-start.21 = (bf16[512,1024]{1,0:T(8,128)(2,1)}, bf16[512,1024]{1,0:T(8,128)(2,1)}, u32[]{:S(2)}, u32[]{:S(2)}) collective-permute-start(bf16[512,1024]{1,0:T(8,128)(2,1)} %pad_maximum_fusion.25), channel_id=1, source_target_pairs={{0,16},{16,0},{8,24},{24,8},{1,17},{17,1},{9,25},{25,9},{2,18},{18... | collective-permute-start | bytes 3145736 | tf_op jit(solution)/shard_map/ppermute | solution.py:414
  213.7 91.4 %collective-permute-start.27 = (bf16[2048,384]{1,0:T(8,128)(2,1)}, bf16[2048,384]{1,0:T(8,128)(2,1)}, u32[]{:S(2)}, u32[]{:S(2)}) collective-permute-start(bf16[2048,384]{1,0:T(8,128)(2,1)} %slice.571), channel_id=1, source_target_pairs={{0,4},{4,0},{1,5},{5,1},{2,6},{6,2},{3,7},{7,3},{8,12},{12,8},{9,1... | collective-permute-start | bytes 4718600 | tf_op jit(solution)/shard_map/ppermute | solution.py:418
  217.9 41.8 %collective-permute-start.22 = (bf16[256,2048]{1,0:T(8,128)(2,1)S(1)}, bf16[256,2048]{1,0:T(8,128)(2,1)}, u32[]{:S(2)}, u32[]{:S(2)}) collective-permute-start(bf16[256,2048]{1,0:T(8,128)(2,1)S(1)} %bitcast.562), channel_id=1, source_target_pairs={{0,16},{16,0},{8,24},{24,8},{1,17},{17,1},{9,25},{25,9},{2,18},{18... | collective-permute-start | bytes 3145736 | tf_op jit(solution)/shard_map/ppermute | solution.py:414
  224.5 75.8 %collective-permute-start.23 = (bf16[256,2048]{1,0:T(8,128)(2,1)}, bf16[256,2048]{1,0:T(8,128)(2,1)}, u32[]{:S(2)}, u32[]{:S(2)}) collective-permute-start(bf16[256,2048]{1,0:T(8,128)(2,1)} %bitcast.68), channel_id=1, source_target_pairs={{0,16},{16,0},{8,24},{24,8},{1,17},{17,1},{9,25},{25,9},{2,18},{18... | collective-permute-start | bytes 3145736 | tf_op jit(solution)/shard_map/ppermute | solution.py:414
  316.7 53.2 %collective-permute-start.26 = (bf16[512,2048]{1,0:T(8,128)(2,1)}, bf16[512,2048]{1,0:T(8,128)(2,1)}, u32[]{:S(2)}, u32[]{:S(2)}) collective-permute-start(bf16[512,2048]{1,0:T(8,128)(2,1)} %convolution_convert_fusion), channel_id=1, source_target_pairs={{0,4},{4,0},{1,5},{5,1},{2,6},{6,2},{3,7},{7,3},{8,12},{12,8},{9,1... | collective-permute-start | bytes 6291464 | tf_op jit(solution)/shard_map/ppermute | solution.py:418
  319.7 26.2 %collective-permute-start.29 = (bf16[256,2048]{1,0:T(8,128)(2,1)}, bf16[256,2048]{1,0:T(8,128)(2,1)S(1)}, u32[]{:S(2)}, u32[]{:S(2)}) collective-permute-start(bf16[256,2048]{1,0:T(8,128)(2,1)} %bitcast.72), channel_id=1, source_target_pairs={{0,16},{16,0},{8,24},{24,8},{1,17},{17,1},{9,25},{25,9},{2,18},{18... | collective-permute-start | bytes 3145736 | tf_op jit(solution)/shard_map/ppermute | solution.py:414
  321.2 47.3 %collective-permute-start.30 = (bf16[256,2048]{1,0:T(8,128)(2,1)}, bf16[256,2048]{1,0:T(8,128)(2,1)}, u32[]{:S(2)}, u32[]{:S(2)}) collective-permute-start(bf16[256,2048]{1,0:T(8,128)(2,1)} %bitcast.73), channel_id=1, source_target_pairs={{0,16},{16,0},{8,24},{24,8},{1,17},{17,1},{9,25},{25,9},{2,18},{18... | collective-permute-start | bytes 3145736 | tf_op jit(solution)/shard_map/ppermute | solution.py:414
  345.9 44.9 %collective-permute-start.31 = (bf16[256,2048]{1,0:T(8,128)(2,1)S(1)}, bf16[256,2048]{1,0:T(8,128)(2,1)S(1)}, u32[]{:S(2)}, u32[]{:S(2)}) collective-permute-start(bf16[256,2048]{1,0:T(8,128)(2,1)S(1)} %bitcast.568), channel_id=1, source_target_pairs={{0,16},{16,0},{8,24},{24,8},{1,17},{17,1},{9,25},{25,9},{2,18},{18... | collective-permute-start | bytes 3145736 | tf_op jit(solution)/shard_map/ppermute | solution.py:414
  368.5 44.8 %collective-permute-start.32 = (bf16[256,2048]{1,0:T(8,128)(2,1)S(1)}, bf16[256,2048]{1,0:T(8,128)(2,1)S(1)}, u32[]{:S(2)}, u32[]{:S(2)}) collective-permute-start(bf16[256,2048]{1,0:T(8,128)(2,1)S(1)} %bitcast.566), channel_id=1, source_target_pairs={{0,16},{16,0},{8,24},{24,8},{1,17},{17,1},{9,25},{25,9},{2,18},{18... | collective-permute-start | bytes 3145736 | tf_op jit(solution)/shard_map/ppermute | solution.py:414
  384.7 97.6 %collective-permute-start.28 = (bf16[512,2048]{1,0:T(8,128)(2,1)}, bf16[512,2048]{1,0:T(8,128)(2,1)}, u32[]{:S(2)}, u32[]{:S(2)}) collective-permute-start(bf16[512,2048]{1,0:T(8,128)(2,1)} %multiply_convert_fusion), channel_id=1, source_target_pairs={{0,4},{4,0},{1,5},{5,1},{2,6},{6,2},{3,7},{7,3},{8,12},{12,8},{9,1... | collective-permute-start | bytes 6291464 | tf_op jit(solution)/shard_map/ppermute | solution.py:418
  390.8 45.0 %collective-permute-start.33 = (bf16[256,2048]{1,0:T(8,128)(2,1)}, bf16[256,2048]{1,0:T(8,128)(2,1)}, u32[]{:S(2)}, u32[]{:S(2)}) collective-permute-start(bf16[256,2048]{1,0:T(8,128)(2,1)} %bitcast.77), channel_id=1, source_target_pairs={{0,16},{16,0},{8,24},{24,8},{1,17},{17,1},{9,25},{25,9},{2,18},{18... | collective-permute-start | bytes 3145736 | tf_op jit(solution)/shard_map/ppermute | solution.py:414
  414.3 44.1 %collective-permute-start.34 = (bf16[256,2048]{1,0:T(8,128)(2,1)S(1)}, bf16[256,2048]{1,0:T(8,128)(2,1)}, u32[]{:S(2)}, u32[]{:S(2)}) collective-permute-start(bf16[256,2048]{1,0:T(8,128)(2,1)S(1)} %bitcast.564), channel_id=1, source_target_pairs={{0,16},{16,0},{8,24},{24,8},{1,17},{17,1},{9,25},{25,9},{2,18},{18... | collective-permute-start | bytes 3145736 | tf_op jit(solution)/shard_map/ppermute | solution.py:414
  435.9 33.7 %collective-permute-start.37 = (bf16[256,1024]{1,0:T(8,128)(2,1)}, bf16[256,1024]{1,0:T(8,128)(2,1)}, u32[]{:S(2)}, u32[]{:S(2)}) collective-permute-start(bf16[256,1024]{1,0:T(8,128)(2,1)} %bitcast.80), channel_id=1, source_target_pairs={{0,16},{16,0},{8,24},{24,8},{1,17},{17,1},{9,25},{25,9},{2,18},{18... | collective-permute-start | bytes 1572872 | tf_op jit(solution)/shard_map/ppermute | solution.py:414
  459.8 475.2 %reduce-scatter.7.cloned.1.call-start = ((), (), s32[]{:S(2)}) async-start(), calls=%async_computation.6 | async-start | bytes 5242880 | tf_op jit(solution)/shard_map/reduce_scatter | solution.py:486
  462.2 66.0 %collective-permute-start.35 = (bf16[512,2048]{1,0:T(8,128)(2,1)}, bf16[512,2048]{1,0:T(8,128)(2,1)}, u32[]{:S(2)}, u32[]{:S(2)}) collective-permute-start(bf16[512,2048]{1,0:T(8,128)(2,1)} %multiply_convert_fusion), channel_id=1, source_target_pairs={{0,8},{8,0},{16,24},{24,16},{1,9},{9,1},{17,25},{25,17},{2,10},{10... | collective-permute-start | bytes 6291464 | tf_op jit(solution)/shard_map/ppermute | solution.py:410
  469.6 77.2 %collective-permute-start.39 = (bf16[256,1024]{1,0:T(8,128)(2,1)S(1)}, bf16[256,1024]{1,0:T(8,128)(2,1)}, u32[]{:S(2)}, u32[]{:S(2)}) collective-permute-start(bf16[256,1024]{1,0:T(8,128)(2,1)S(1)} %bitcast.590), channel_id=1, source_target_pairs={{0,16},{16,0},{8,24},{24,8},{1,17},{17,1},{9,25},{25,9},{2,18},{18... | collective-permute-start | bytes 1572872 | tf_op jit(solution)/shard_map/ppermute | solution.py:414
  480.8 67.8 %collective-permute-start.40 = (bf16[256,1024]{1,0:T(8,128)(2,1)S(1)}, bf16[256,1024]{1,0:T(8,128)(2,1)}, u32[]{:S(2)}, u32[]{:S(2)}) collective-permute-start(bf16[256,1024]{1,0:T(8,128)(2,1)S(1)} %bitcast.588), channel_id=1, source_target_pairs={{0,16},{16,0},{8,24},{24,8},{1,17},{17,1},{9,25},{25,9},{2,18},{18... | collective-permute-start | bytes 1572872 | tf_op jit(solution)/shard_map/ppermute | solution.py:414
  528.2 30.8 %collective-permute-start.36 = (bf16[512,2048]{1,0:T(8,128)(2,1)}, bf16[512,2048]{1,0:T(8,128)(2,1)S(1)}, u32[]{:S(2)}, u32[]{:S(2)}) collective-permute-start(bf16[512,2048]{1,0:T(8,128)(2,1)} %collective-permute-done.35), channel_id=1, source_target_pairs={{0,4},{4,0},{1,5},{5,1},{2,6},{6,2},{3,7},{7,3},{8,12},{12,8},{9,1... | collective-permute-start | bytes 6291464 | tf_op jit(solution)/shard_map/ppermute | solution.py:418
  602.4 47.7 %collective-permute-start.43 = (bf16[512,2048]{1,0:T(8,128)(2,1)S(1)}, bf16[512,2048]{1,0:T(8,128)(2,1)S(1)}, u32[]{:S(2)}, u32[]{:S(2)}) collective-permute-start(bf16[512,2048]{1,0:T(8,128)(2,1)S(1)} %add_convert_fusion.12), channel_id=1, source_target_pairs={{0,8},{8,0},{16,24},{24,16},{1,9},{9,1},{17,25},{25,17},{2,10},{10... | collective-permute-start | bytes 6291464 | tf_op jit(solution)/shard_map/ppermute | solution.py:410
  611.3 38.8 %collective-permute-start.42 = (bf16[512,2048]{1,0:T(8,128)(2,1)S(1)}, bf16[512,2048]{1,0:T(8,128)(2,1)S(1)}, u32[]{:S(2)}, u32[]{:S(2)}) collective-permute-start(bf16[512,2048]{1,0:T(8,128)(2,1)S(1)} %convolution_convert_fusion.1), channel_id=1, source_target_pairs={{0,4},{4,0},{1,5},{5,1},{2,6},{6,2},{3,7},{7,3},{8,12},{12,8},{9,1... | collective-permute-start | bytes 6291464 | tf_op jit(solution)/shard_map/ppermute | solution.py:418
  673.8 48.2 %collective-permute-start.45 = (bf16[512,2048]{1,0:T(8,128)(2,1)}, bf16[512,2048]{1,0:T(8,128)(2,1)S(1)}, u32[]{:S(2)}, u32[]{:S(2)}) collective-permute-start(bf16[512,2048]{1,0:T(8,128)(2,1)} %fusion.52), channel_id=1, source_target_pairs={{0,8},{8,0},{16,24},{24,16},{1,9},{9,1},{17,25},{25,17},{2,10},{10... | collective-permute-start | bytes 6291464 | tf_op jit(solution)/shard_map/ppermute | solution.py:410
  784.7 266.0 %reduce-scatter.9.cloned.1.call-start = ((), (), s32[]{:S(2)}) async-start(), calls=%async_computation.7 | async-start | bytes 2621440 | tf_op jit(solution)/shard_map/reduce_scatter | solution.py:486
  784.8 52.6 %collective-permute-start.53 = (bf16[256,1024]{1,0:T(8,128)(2,1)S(1)}, bf16[256,1024]{1,0:T(8,128)(2,1)S(1)}, u32[]{:S(2)}, u32[]{:S(2)}) collective-permute-start(bf16[256,1024]{1,0:T(8,128)(2,1)S(1)} %get-tuple-element.277), channel_id=1, source_target_pairs={{0,16},{16,0},{8,24},{24,8},{1,17},{17,1},{9,25},{25,9},{2,18},{18... | collective-permute-start | bytes 1572872 | tf_op jit(solution)/shard_map/ppermute | solution.py:414
  835.4 95.5 %collective-permute-start.48 = (bf16[512,2048]{1,0:T(8,128)(2,1)}, bf16[512,2048]{1,0:T(8,128)(2,1)S(1)}, u32[]{:S(2)}, u32[]{:S(2)}) collective-permute-start(bf16[512,2048]{1,0:T(8,128)(2,1)} %add_convert_fusion.9), channel_id=1, source_target_pairs={{0,4},{4,0},{1,5},{5,1},{2,6},{6,2},{3,7},{7,3},{8,12},{12,8},{9,1... | collective-permute-start | bytes 6291464 | tf_op jit(solution)/shard_map/ppermute | solution.py:418
  836.3 44.6 %collective-permute-start.49 = (bf16[256,1024]{1,0:T(8,128)(2,1)S(1)}, bf16[256,1024]{1,0:T(8,128)(2,1)S(1)}, u32[]{:S(2)}, u32[]{:S(2)}) collective-permute-start(bf16[256,1024]{1,0:T(8,128)(2,1)S(1)} %get-tuple-element.136), channel_id=1, source_target_pairs={{0,16},{16,0},{8,24},{24,8},{1,17},{17,1},{9,25},{25,9},{2,18},{18... | collective-permute-start | bytes 1572872 | tf_op jit(solution)/shard_map/ppermute | solution.py:414
  837.4 44.6 %collective-permute-start.54 = (bf16[256,1024]{1,0:T(8,128)(2,1)S(1)}, bf16[256,1024]{1,0:T(8,128)(2,1)S(1)}, u32[]{:S(2)}, u32[]{:S(2)}) collective-permute-start(bf16[256,1024]{1,0:T(8,128)(2,1)S(1)} %get-tuple-element.140), channel_id=1, source_target_pairs={{0,16},{16,0},{8,24},{24,8},{1,17},{17,1},{9,25},{25,9},{2,18},{18... | collective-permute-start | bytes 1572872 | tf_op jit(solution)/shard_map/ppermute | solution.py:414
  880.9 48.6 %collective-permute-start.50 = (bf16[256,2048]{1,0:T(8,128)(2,1)S(1)}, bf16[256,2048]{1,0:T(8,128)(2,1)S(1)}, u32[]{:S(2)}, u32[]{:S(2)}) collective-permute-start(bf16[256,2048]{1,0:T(8,128)(2,1)S(1)} %get-tuple-element.137), channel_id=1, source_target_pairs={{0,16},{16,0},{8,24},{24,8},{1,17},{17,1},{9,25},{25,9},{2,18},{18... | collective-permute-start | bytes 3145736 | tf_op jit(solution)/shard_map/ppermute | solution.py:414
  882.0 45.9 %collective-permute-start.55 = (bf16[256,2048]{1,0:T(8,128)(2,1)S(1)}, bf16[256,2048]{1,0:T(8,128)(2,1)S(1)}, u32[]{:S(2)}, u32[]{:S(2)}) collective-permute-start(bf16[256,2048]{1,0:T(8,128)(2,1)S(1)} %get-tuple-element.142), channel_id=1, source_target_pairs={{0,16},{16,0},{8,24},{24,8},{1,17},{17,1},{9,25},{25,9},{2,18},{18... | collective-permute-start | bytes 3145736 | tf_op jit(solution)/shard_map/ppermute | solution.py:414
  927.9 29.2 %collective-permute-start.57 = (bf16[256,2048]{1,0:T(8,128)(2,1)}, bf16[256,2048]{1,0:T(8,128)(2,1)}, u32[]{:S(2)}, u32[]{:S(2)}) collective-permute-start(bf16[256,2048]{1,0:T(8,128)(2,1)} %get-tuple-element.144), channel_id=1, source_target_pairs={{0,16},{16,0},{8,24},{24,8},{1,17},{17,1},{9,25},{25,9},{2,18},{18... | collective-permute-start | bytes 3145736 | tf_op jit(solution)/shard_map/ppermute | solution.py:414
  930.5 46.3 %collective-permute-start.56 = (bf16[256,2048]{1,0:T(8,128)(2,1)}, bf16[256,2048]{1,0:T(8,128)(2,1)}, u32[]{:S(2)}, u32[]{:S(2)}) collective-permute-start(bf16[256,2048]{1,0:T(8,128)(2,1)} %get-tuple-element.143), channel_id=1, source_target_pairs={{0,16},{16,0},{8,24},{24,8},{1,17},{17,1},{9,25},{25,9},{2,18},{18... | collective-permute-start | bytes 3145736 | tf_op jit(solution)/shard_map/ppermute | solution.py:414
  933.5 46.1 %collective-permute-start.52 = (bf16[512,2048]{1,0:T(8,128)(2,1)}, bf16[512,2048]{1,0:T(8,128)(2,1)S(1)}, u32[]{:S(2)}, u32[]{:S(2)}) collective-permute-start(bf16[512,2048]{1,0:T(8,128)(2,1)} %add_convert_fusion.8), channel_id=1, source_target_pairs={{0,8},{8,0},{16,24},{24,16},{1,9},{9,1},{17,25},{25,17},{2,10},{10... | collective-permute-start | bytes 6291464 | tf_op jit(solution)/shard_map/ppermute | solution.py:410
  946.2 44.2 %collective-permute-start.51 = (bf16[512,2048]{1,0:T(8,128)(2,1)}, bf16[512,2048]{1,0:T(8,128)(2,1)}, u32[]{:S(2)}, u32[]{:S(2)}) collective-permute-start(bf16[512,2048]{1,0:T(8,128)(2,1)} %add_convert_fusion.7), channel_id=1, source_target_pairs={{0,4},{4,0},{1,5},{5,1},{2,6},{6,2},{3,7},{7,3},{8,12},{12,8},{9,1... | collective-permute-start | bytes 6291464 | tf_op jit(solution)/shard_map/ppermute | solution.py:418
  956.9 338.4 %reduce-scatter.17.cloned.1.call-start = ((), (), s32[]{:S(2)}) async-start(), calls=%async_computation.11 | async-start | bytes 5242880 | tf_op jit(solution)/shard_map/reduce_scatter | solution.py:486
  957.2 64.8 %collective-permute-start.59 = (bf16[256,2048]{1,0:T(8,128)(2,1)}, bf16[256,2048]{1,0:T(8,128)(2,1)}, u32[]{:S(2)}, u32[]{:S(2)}) collective-permute-start(bf16[256,2048]{1,0:T(8,128)(2,1)} %get-tuple-element.146), channel_id=1, source_target_pairs={{0,16},{16,0},{8,24},{24,8},{1,17},{17,1},{9,25},{25,9},{2,18},{18... | collective-permute-start | bytes 3145736 | tf_op jit(solution)/shard_map/ppermute | solution.py:414
  976.8 46.9 %collective-permute-start.64 = (bf16[256,2048]{1,0:T(8,128)(2,1)}, bf16[256,2048]{1,0:T(8,128)(2,1)}, u32[]{:S(2)}, u32[]{:S(2)}) collective-permute-start(bf16[256,2048]{1,0:T(8,128)(2,1)} %get-tuple-element.150), channel_id=1, source_target_pairs={{0,16},{16,0},{8,24},{24,8},{1,17},{17,1},{9,25},{25,9},{2,18},{18... | collective-permute-start | bytes 3145736 | tf_op jit(solution)/shard_map/ppermute | solution.py:414
  1009.4 25.7 %collective-permute-start.58 = (bf16[512,2048]{1,0:T(8,128)(2,1)}, bf16[512,2048]{1,0:T(8,128)(2,1)}, u32[]{:S(2)}, u32[]{:S(2)}) collective-permute-start(bf16[512,2048]{1,0:T(8,128)(2,1)} %pad_maximum_fusion.14), channel_id=1, source_target_pairs={{0,4},{4,0},{1,5},{5,1},{2,6},{6,2},{3,7},{7,3},{8,12},{12,8},{9,1... | collective-permute-start | bytes 6291464 | tf_op jit(solution)/shard_map/ppermute | solution.py:418
  1021.9 335.9 %reduce-scatter.11.cloned.1.call-start = ((), (), s32[]{:S(2)}) async-start(), calls=%async_computation.8 | async-start | bytes 1966080 | tf_op jit(solution)/shard_map/reduce_scatter | solution.py:486
  1022.0 101.5 %collective-permute-start.66 = (bf16[256,2048]{1,0:T(8,128)(2,1)}, bf16[256,2048]{1,0:T(8,128)(2,1)}, u32[]{:S(2)}, u32[]{:S(2)}) collective-permute-start(bf16[256,2048]{1,0:T(8,128)(2,1)} %get-tuple-element.153), channel_id=1, source_target_pairs={{0,16},{16,0},{8,24},{24,8},{1,17},{17,1},{9,25},{25,9},{2,18},{18... | collective-permute-start | bytes 3145736 | tf_op jit(solution)/shard_map/ppermute | solution.py:414
  1023.8 99.7 %collective-permute-start.65 = (bf16[256,2048]{1,0:T(8,128)(2,1)}, bf16[256,2048]{1,0:T(8,128)(2,1)}, u32[]{:S(2)}, u32[]{:S(2)}) collective-permute-start(bf16[256,2048]{1,0:T(8,128)(2,1)} %get-tuple-element.152), channel_id=1, source_target_pairs={{0,16},{16,0},{8,24},{24,8},{1,17},{17,1},{9,25},{25,9},{2,18},{18... | collective-permute-start | bytes 3145736 | tf_op jit(solution)/shard_map/ppermute | solution.py:414
  1113.0 34.0 %collective-permute-start.62 = (bf16[256,1024]{1,0:T(8,128)(2,1)}, bf16[256,1024]{1,0:T(8,128)(2,1)}, u32[]{:S(2)}, u32[]{:S(2)}) collective-permute-start(bf16[256,1024]{1,0:T(8,128)(2,1)} %get-tuple-element.148), channel_id=1, source_target_pairs={{0,8},{8,0},{16,24},{24,16},{1,9},{9,1},{17,25},{25,17},{2,10},{10... | collective-permute-start | bytes 1572872 | tf_op jit(solution)/shard_map/ppermute | solution.py:410
  1114.5 32.4 %collective-permute-start.63 = (bf16[256,1024]{1,0:T(8,128)(2,1)}, bf16[256,1024]{1,0:T(8,128)(2,1)}, u32[]{:S(2)}, u32[]{:S(2)}) collective-permute-start(bf16[256,1024]{1,0:T(8,128)(2,1)} %get-tuple-element.149), channel_id=1, source_target_pairs={{0,8},{8,0},{16,24},{24,16},{1,9},{9,1},{17,25},{25,17},{2,10},{10... | collective-permute-start | bytes 1572872 | tf_op jit(solution)/shard_map/ppermute | solution.py:410
  1158.3 38.0 %collective-permute-start.78 = (bf16[2048,384]{1,0:T(8,128)(2,1)}, bf16[2048,384]{1,0:T(8,128)(2,1)}, u32[]{:S(2)}, u32[]{:S(2)}) collective-permute-start(bf16[2048,384]{1,0:T(8,128)(2,1)} %bitcast.592), channel_id=1, source_target_pairs={{0,4},{4,0},{1,5},{5,1},{2,6},{6,2},{3,7},{7,3},{8,12},{12,8},{9,1... | collective-permute-start | bytes 4718600 | tf_op jit(solution)/shard_map/ppermute | solution.py:418
  1158.4 28.7 %collective-permute-start.70 = (bf16[256,1536]{1,0:T(8,128)(2,1)}, bf16[256,1536]{1,0:T(8,128)(2,1)S(1)}, u32[]{:S(2)}, u32[]{:S(2)}) collective-permute-start(bf16[256,1536]{1,0:T(8,128)(2,1)} %get-tuple-element.157), channel_id=1, source_target_pairs={{0,8},{8,0},{16,24},{24,16},{1,9},{9,1},{17,25},{25,17},{2,10},{10... | collective-permute-start | bytes 2359304 | tf_op jit(solution)/shard_map/ppermute | solution.py:410
  1162.8 28.0 %collective-permute-start.72 = (bf16[256,1024]{1,0:T(8,128)(2,1)S(1)}, bf16[256,1024]{1,0:T(8,128)(2,1)S(1)}, u32[]{:S(2)}, u32[]{:S(2)}) collective-permute-start(bf16[256,1024]{1,0:T(8,128)(2,1)S(1)} %get-tuple-element.160), channel_id=1, source_target_pairs={{0,16},{16,0},{8,24},{24,8},{1,17},{17,1},{9,25},{25,9},{2,18},{18... | collective-permute-start | bytes 1572872 | tf_op jit(solution)/shard_map/ppermute | solution.py:414
  1164.6 29.6 %collective-permute-start.74 = (bf16[256,1024]{1,0:T(8,128)(2,1)}, bf16[256,1024]{1,0:T(8,128)(2,1)}, u32[]{:S(2)}, u32[]{:S(2)}) collective-permute-start(bf16[256,1024]{1,0:T(8,128)(2,1)} %get-tuple-element.162), channel_id=1, source_target_pairs={{0,16},{16,0},{8,24},{24,8},{1,17},{17,1},{9,25},{25,9},{2,18},{18... | collective-permute-start | bytes 1572872 | tf_op jit(solution)/shard_map/ppermute | solution.py:414
  1194.2 31.4 %collective-permute-start.75 = (bf16[256,1536]{1,0:T(8,128)(2,1)}, bf16[256,1536]{1,0:T(8,128)(2,1)S(1)}, u32[]{:S(2)}, u32[]{:S(2)}) collective-permute-start(bf16[256,1536]{1,0:T(8,128)(2,1)} %get-tuple-element.163), channel_id=1, source_target_pairs={{0,16},{16,0},{8,24},{24,8},{1,17},{17,1},{9,25},{25,9},{2,18},{18... | collective-permute-start | bytes 2359304 | tf_op jit(solution)/shard_map/ppermute | solution.py:414
  1198.2 33.9 %collective-permute-start.71 = (bf16[256,1536]{1,0:T(8,128)(2,1)S(1)}, bf16[256,1536]{1,0:T(8,128)(2,1)S(1)}, u32[]{:S(2)}, u32[]{:S(2)}) collective-permute-start(bf16[256,1536]{1,0:T(8,128)(2,1)S(1)} %copy-done.115), channel_id=1, source_target_pairs={{0,8},{8,0},{16,24},{24,16},{1,9},{9,1},{17,25},{25,17},{2,10},{10... | collective-permute-start | bytes 2359304 | tf_op jit(solution)/shard_map/ppermute | solution.py:410
  1198.6 46.4 %collective-permute-start.79 = (bf16[2,512,384]{2,1,0:T(8,128)(2,1)S(1)}, bf16[2,512,384]{2,1,0:T(8,128)(2,1)}, u32[]{:S(2)}, u32[]{:S(2)}) collective-permute-start(bf16[2,512,384]{2,1,0:T(8,128)(2,1)S(1)} %dynamic-slice_bitcast_fusion), channel_id=1, source_target_pairs={{0,8},{8,0},{16,24},{24,16},{1,9},{9,1},{17,25},{25,17},{2,10},{10... | collective-permute-start | bytes 2359304 | tf_op jit(solution)/shard_map/ppermute | solution.py:410
  1236.2 123.9 %reduce-scatter.13.cloned.1.call-start = ((), (), s32[]{:S(2)}) async-start(), calls=%async_computation.9 | async-start | bytes 5242880 | tf_op jit(solution)/shard_map/reduce_scatter | solution.py:486
  1266.1 126.8 %reduce-scatter.15.cloned.1.call-start = ((), (), s32[]{:S(2)}) async-start(), calls=%async_computation.10 | async-start | bytes 1310720 | tf_op jit(solution)/shard_map/reduce_scatter | solution.py:486
  1297.2 31.1 %collective-permute-start.85 = (bf16[2,64,2048]{2,1,0:T(8,128)(2,1)}, bf16[2,64,2048]{2,1,0:T(8,128)(2,1)}, u32[]{:S(2)}, u32[]{:S(2)}) collective-permute-start(bf16[2,64,2048]{2,1,0:T(8,128)(2,1)} %dynamic-slice_bitcast_fusion.2), channel_id=1, source_target_pairs={{0,8},{8,0},{16,24},{24,16},{1,9},{9,1},{17,25},{25,17},{2,10},{10... | collective-permute-start | bytes 1572872 | tf_op jit(solution)/shard_map/ppermute | solution.py:410
  1313.7 36.7 %collective-permute-start.90 = (bf16[2,64,2048]{2,1,0:T(8,128)(2,1)}, bf16[2,64,2048]{2,1,0:T(8,128)(2,1)}, u32[]{:S(2)}, u32[]{:S(2)}) collective-permute-start(bf16[2,64,2048]{2,1,0:T(8,128)(2,1)} %fusion.266), channel_id=1, source_target_pairs={{0,8},{8,0},{16,24},{24,16},{1,9},{9,1},{17,25},{25,17},{2,10},{10... | collective-permute-start | bytes 1572872 | tf_op jit(solution)/shard_map/ppermute | solution.py:410
  (281 other events, 4896.1 us)
Sparse Core Ops, SparseCore 0:
  16.8 46.1 all-gather.14
  64.5 32.9 all-gather.12
  99.1 79.2 all-gather.16
  179.8 79.2 all-gather.18
  260.6 44.4 all-gather.20
  460.0 80.1 all-gather.22
  784.8 74.3 reduce-scatter.6
  957.0 41.5 reduce-scatter.8
  1022.0 75.4 reduce-scatter.16
  1236.3 40.2 reduce-scatter.10
  1278.9 81.1 reduce-scatter.12
  1365.1 27.8 reduce-scatter.14
